TPU v7x, 32 devices: a whole 2x2x4 slice. The times are simulated.
32 devices in a mesh: row: 8 (over z, x), col: 4 (over y, core).
Axes of the slice: x: 2, y: 2, z: 4, core: 2. Of those that a mesh axis runs over, the one named last changes fastest.
Arguments:
- tokens: bfloat16 [4096, 4096], P('row', 'col'), may hold values from -6 to 6
- gate_weight: bfloat16 [4096, 16384], P('row', 'col'), may hold values from -0.125 to 0.125
- up_weight: bfloat16 [4096, 16384], P('row', 'col'), may hold values from -0.125 to 0.125
- tile_mask: int32 [32, 128], P(None, 'col'), may hold values from 0 to 1, as said below
Outputs:
- hidden: bfloat16 [4096, 16384], P('row', 'col')
Inputs may be any that keep to these rules, and one draw needn't show every extreme that they name: `tile_mask`: values are 0 or 1. In each aligned block of 4 x 32 tiles (tile rows r * 4 to (r + 1) * 4 - 1, tile columns c * 32 to (c + 1) * 32 - 1) at least 48 and at most 80 tiles are kept; some block keeps exactly 80.
All inputs are finite; a program needn't handle non-finite values.
Results may differ from a plain program's by a relative error of at most 0.001.
Values may be sent and summed in bfloat16 or wider, within the bound.
A program may use at most 128 MiB of HBM per device.

v0:
```python
import jax
import jax.numpy as jnp
from jax import lax
from jax.sharding import PartitionSpec as P

TILE = 128


def passed_along(value, axis, steps):
    count = lax.axis_size(axis)
    pairs = [(source, (source + steps) % count) for source in range(count)]
    return lax.ppermute(value, axis, pairs)


def selector(mask_rows, slot_count):
    flat_mask = mask_rows.reshape(-1)
    position = jnp.cumsum(flat_mask) - 1
    slot_ids = jnp.arange(slot_count, dtype=jnp.int32)
    hits = (position[None, :] == slot_ids[:, None]) & (flat_mask[None, :] == 1)
    return hits.astype(jnp.bfloat16)


def on_device(tokens, gate_weight, up_weight, tile_mask):
    rows_here = gate_weight.shape[0]
    cols_here = gate_weight.shape[1]
    row_tiles = rows_here // TILE
    col_tiles = cols_here // TILE
    slot_count = 5 * row_tiles * col_tiles // 8
    row_count = lax.axis_size("row")
    row_index = lax.axis_index("row")
    whole_rows = lax.all_gather(tokens, "col", axis=1, tiled=True)

    def mask_block(block_index):
        return lax.dynamic_slice_in_dim(tile_mask, block_index * row_tiles, row_tiles, 0)

    own_mask = mask_block(row_index)
    own_select = selector(own_mask, slot_count)

    def pack_tiles(weight):
        pieces = weight.reshape(row_tiles, TILE, col_tiles, TILE).transpose(0, 2, 1, 3)
        pieces = pieces.reshape(row_tiles * col_tiles, TILE, TILE)
        packed = jnp.einsum("st,tde->sde", own_select, pieces, preferred_element_type=jnp.float32)
        return packed.astype(jnp.bfloat16)

    own_block = jnp.stack([pack_tiles(gate_weight), pack_tiles(up_weight)])

    def unpack_pair(buffer, block_index):
        chosen = selector(mask_block(block_index), slot_count)
        dense_cells = jnp.einsum(
            "st,gsde->gtde", chosen, buffer, preferred_element_type=jnp.float32
        )
        dense_cells = dense_cells.astype(jnp.bfloat16).reshape(2, row_tiles, col_tiles, TILE, TILE)
        dense_cells = dense_cells.transpose(0, 1, 3, 2, 4).reshape(2, rows_here, cols_here)
        return (dense_cells[0], dense_cells[1])

    def add_block(totals, buffer, block_index):
        columns = lax.dynamic_slice_in_dim(whole_rows, block_index * rows_here, rows_here, 1)
        gate_piece, up_piece = unpack_pair(buffer, block_index)
        gate_next = totals[0] + jnp.dot(columns, gate_piece, preferred_element_type=jnp.float32)
        up_next = totals[1] + jnp.dot(columns, up_piece, preferred_element_type=jnp.float32)
        return (gate_next, up_next)

    zeros_acc = jnp.zeros((whole_rows.shape[0], cols_here), jnp.float32)
    own_total = add_block((zeros_acc, zeros_acc), own_block, row_index)

    def advance_one(offset, state_now):
        totals, held_block = state_now
        held_block = passed_along(held_block, "row", 1)
        totals = add_block(totals, held_block, (row_index - offset) % row_count)
        return (totals, held_block)

    totals, held_block = lax.fori_loop(1, row_count, advance_one, (own_total, own_block))
    gate_sum, up_sum = totals
    return (jax.nn.silu(gate_sum) * up_sum).astype(jnp.bfloat16)


def solution(mesh):
    placed = (P("row", "col"), P("row", "col"), P("row", "col"), P(None, "col"))
    return jax.shard_map(
        on_device, mesh=mesh, in_specs=placed, out_specs=P("row", "col"), check_vma=False
    )
```

profile of v0, /device:TPU:1, one launch (start us, length us, event | category | flops | bytes accessed | tf_op | source)
XLA Modules:
  0.0 1198.1 jit_solution(12519393166619736774)
XLA Ops:
  8.3 3.4 copy.19
  12.7 1.3 copy.12
  17.0 1.3 copy.13
  20.2 4.7 convolution_convert_fusion.1
  24.9 8.4 copy.42
  33.3 5.0 pad_maximum_fusion
  39.4 4.1 fusion.36
  43.5 2.4 all-gather.2.cloned.1.call-done
  45.9 8.2 fusion.16
  54.1 6.7 fusion.13
  60.8 1121.7 %while.19 = (s32[]{:T(128)}, f32[512,4096]{1,0:T(8,128)}, f32[512,4096]{1,0:T(8,128)}, bf16[2,80,128,128]{3,1,2,0:T(8,128)(2,1)}, s32[]{:T(128)}, /*index=5*/bf1...) while((s32[]{:T(128)}, f32[512,4096]{1,0:T(8,128)}, ...), condition=%wide.region_3.4_spmd, body=%wide.region_1.3_spmd.sunk | while | flops 4974481408 | bytes 239081040 | solution.py:72
  63.2 115.0 %collective-permute-done = bf16[2,80,128,128]{3,1,2,0:T(8,128)(2,1)} collective-permute-done((bf16[2,80,128,128]{3,1,2,0:T(8,128)(2,1)}, bf16[2,80,128,128]{3,1,2,0:T(8,128)(2,1)}, u32[]{:S(2)}, u32[]{:S(2)}) %collective-permute-start) | collective-permute-done | bytes 5242912 | tf_op jit(solution)/shard_map/while/body/eval_jaxpr/ppermute | solution.py:12
  178.2 8.1 convolution_convert_fusion.3
  186.3 8.4 copy.48
  194.7 4.3 fusion.53
  200.6 7.1 convolution_add_fusion.5
  207.7 7.4 convolution_add_fusion.4
  215.1 8.7 copy.60
  225.0 115.3 %collective-permute-done = bf16[2,80,128,128]{3,1,2,0:T(8,128)(2,1)} collective-permute-done((bf16[2,80,128,128]{3,1,2,0:T(8,128)(2,1)}, bf16[2,80,128,128]{3,1,2,0:T(8,128)(2,1)}, u32[]{:S(2)}, u32[]{:S(2)}) %collective-permute-start) | collective-permute-done | bytes 5242912 | tf_op jit(solution)/shard_map/while/body/eval_jaxpr/ppermute | solution.py:12
  340.3 8.1 convolution_convert_fusion.3
  348.4 8.4 copy.48
  356.8 4.3 fusion.53
  361.4 1.3 slice-done.3
  362.7 7.1 convolution_add_fusion.5
  369.8 7.4 convolution_add_fusion.4
  377.2 8.7 copy.60
  387.1 114.4 %collective-permute-done = bf16[2,80,128,128]{3,1,2,0:T(8,128)(2,1)} collective-permute-done((bf16[2,80,128,128]{3,1,2,0:T(8,128)(2,1)}, bf16[2,80,128,128]{3,1,2,0:T(8,128)(2,1)}, u32[]{:S(2)}, u32[]{:S(2)}) %collective-permute-start) | collective-permute-done | bytes 5242912 | tf_op jit(solution)/shard_map/while/body/eval_jaxpr/ppermute | solution.py:12
  501.5 8.1 convolution_convert_fusion.3
  509.6 8.4 copy.48
  517.9 4.3 fusion.53
  522.6 1.3 slice-done.3
  523.9 7.1 convolution_add_fusion.5
  531.0 7.4 convolution_add_fusion.4
  538.4 8.7 copy.60
  548.3 113.5 %collective-permute-done = bf16[2,80,128,128]{3,1,2,0:T(8,128)(2,1)} collective-permute-done((bf16[2,80,128,128]{3,1,2,0:T(8,128)(2,1)}, bf16[2,80,128,128]{3,1,2,0:T(8,128)(2,1)}, u32[]{:S(2)}, u32[]{:S(2)}) %collective-permute-start) | collective-permute-done | bytes 5242912 | tf_op jit(solution)/shard_map/while/body/eval_jaxpr/ppermute | solution.py:12
  661.8 8.1 convolution_convert_fusion.3
  669.8 8.4 copy.48
  678.2 4.3 fusion.53
  682.9 1.3 slice-done.3
  684.1 7.1 convolution_add_fusion.5
  691.2 7.4 convolution_add_fusion.4
  698.6 8.7 copy.60
  708.5 112.5 %collective-permute-done = bf16[2,80,128,128]{3,1,2,0:T(8,128)(2,1)} collective-permute-done((bf16[2,80,128,128]{3,1,2,0:T(8,128)(2,1)}, bf16[2,80,128,128]{3,1,2,0:T(8,128)(2,1)}, u32[]{:S(2)}, u32[]{:S(2)}) %collective-permute-start) | collective-permute-done | bytes 5242912 | tf_op jit(solution)/shard_map/while/body/eval_jaxpr/ppermute | solution.py:12
  821.1 8.1 convolution_convert_fusion.3
  829.1 8.4 copy.48
  837.5 4.3 fusion.53
  843.4 7.1 convolution_add_fusion.5
  850.6 7.4 convolution_add_fusion.4
  858.0 8.7 copy.60
  867.8 111.6 %collective-permute-done = bf16[2,80,128,128]{3,1,2,0:T(8,128)(2,1)} collective-permute-done((bf16[2,80,128,128]{3,1,2,0:T(8,128)(2,1)}, bf16[2,80,128,128]{3,1,2,0:T(8,128)(2,1)}, u32[]{:S(2)}, u32[]{:S(2)}) %collective-permute-start) | collective-permute-done | bytes 5242912 | tf_op jit(solution)/shard_map/while/body/eval_jaxpr/ppermute | solution.py:12
  979.5 8.1 convolution_convert_fusion.3
  987.5 8.4 copy.48
  995.9 4.3 fusion.53
  1001.9 7.1 convolution_add_fusion.5
  1009.0 7.4 convolution_add_fusion.4
  1016.4 8.7 copy.60
  1026.3 110.7 %collective-permute-done = bf16[2,80,128,128]{3,1,2,0:T(8,128)(2,1)} collective-permute-done((bf16[2,80,128,128]{3,1,2,0:T(8,128)(2,1)}, bf16[2,80,128,128]{3,1,2,0:T(8,128)(2,1)}, u32[]{:S(2)}, u32[]{:S(2)}) %collective-permute-start) | collective-permute-done | bytes 5242912 | tf_op jit(solution)/shard_map/while/body/eval_jaxpr/ppermute | solution.py:12
  1137.0 8.1 convolution_convert_fusion.3
  1145.0 8.4 copy.48
  1153.4 4.3 fusion.53
  1159.3 7.1 convolution_add_fusion.5
  1166.4 7.4 convolution_add_fusion.4
  1173.8 8.7 copy.60
  1182.6 8.8 multiply_convert_fusion
  (157 shorter events, 25.1 us)
Async XLA Ops:
  6.5 39.4 %all-gather.2.cloned.1.call-start = ((), (), s32[]{:S(2)}) async-start(), calls=%async_computation | async-start | bytes 5242880 | tf_op jit(solution)/shard_map/all_gather | solution.py:31
  12.7 2.2 copy-start.5
  20.2 4.8 copy-start.3
  33.3 6.1 copy-start.2
  45.9 8.2 copy-start.4
  60.8 117.4 %collective-permute-start = (bf16[2,80,128,128]{3,1,2,0:T(8,128)(2,1)}, bf16[2,80,128,128]{3,1,2,0:T(8,128)(2,1)}, u32[]{:S(2)}, u32[]{:S(2)}) collective-permute-start(bf16[2,80,128,128]{3,1,2,0:T(8,128)(2,1)} %get-tuple-element.277), channel_id=1, source_target_pairs={{0,4},{4,8},{8,12},{12,16},{16,20},{20,24},{24,28},{28,0},{1,5},{5... | collective-permute-start | bytes 15728648 | tf_op jit(solution)/shard_map/while/body/eval_jaxpr/ppermute | solution.py:12
  194.7 4.7 slice-start.2
  194.7 5.9 slice-start.3
  199.0 8.7 slice-start
  200.6 7.1 slice-start.1
  207.7 7.4 copy-start.1
  215.1 8.7 copy-start
  223.8 116.5 %collective-permute-start = (bf16[2,80,128,128]{3,1,2,0:T(8,128)(2,1)}, bf16[2,80,128,128]{3,1,2,0:T(8,128)(2,1)}, u32[]{:S(2)}, u32[]{:S(2)}) collective-permute-start(bf16[2,80,128,128]{3,1,2,0:T(8,128)(2,1)} %get-tuple-element.277), channel_id=1, source_target_pairs={{0,4},{4,8},{8,12},{12,16},{16,20},{20,24},{24,28},{28,0},{1,5},{5... | collective-permute-start | bytes 15728648 | tf_op jit(solution)/shard_map/while/body/eval_jaxpr/ppermute | solution.py:12
  356.8 4.7 slice-start.2
  356.8 5.9 slice-start.3
  361.1 8.7 slice-start
  362.7 7.1 slice-start.1
  369.8 7.4 copy-start.1
  377.2 8.7 copy-start
  385.9 115.6 %collective-permute-start = (bf16[2,80,128,128]{3,1,2,0:T(8,128)(2,1)}, bf16[2,80,128,128]{3,1,2,0:T(8,128)(2,1)}, u32[]{:S(2)}, u32[]{:S(2)}) collective-permute-start(bf16[2,80,128,128]{3,1,2,0:T(8,128)(2,1)} %get-tuple-element.277), channel_id=1, source_target_pairs={{0,4},{4,8},{8,12},{12,16},{16,20},{20,24},{24,28},{28,0},{1,5},{5... | collective-permute-start | bytes 15728648 | tf_op jit(solution)/shard_map/while/body/eval_jaxpr/ppermute | solution.py:12
  517.9 4.7 slice-start.2
  517.9 5.9 slice-start.3
  522.3 8.7 slice-start
  523.9 7.1 slice-start.1
  531.0 7.4 copy-start.1
  538.4 8.7 copy-start
  547.1 114.7 %collective-permute-start = (bf16[2,80,128,128]{3,1,2,0:T(8,128)(2,1)}, bf16[2,80,128,128]{3,1,2,0:T(8,128)(2,1)}, u32[]{:S(2)}, u32[]{:S(2)}) collective-permute-start(bf16[2,80,128,128]{3,1,2,0:T(8,128)(2,1)} %get-tuple-element.277), channel_id=1, source_target_pairs={{0,4},{4,8},{8,12},{12,16},{16,20},{20,24},{24,28},{28,0},{1,5},{5... | collective-permute-start | bytes 15728648 | tf_op jit(solution)/shard_map/while/body/eval_jaxpr/ppermute | solution.py:12
  678.2 4.7 slice-start.2
  678.2 5.9 slice-start.3
  682.6 8.6 slice-start
  684.1 7.1 slice-start.1
  691.2 7.4 copy-start.1
  698.6 8.7 copy-start
  707.3 113.7 %collective-permute-start = (bf16[2,80,128,128]{3,1,2,0:T(8,128)(2,1)}, bf16[2,80,128,128]{3,1,2,0:T(8,128)(2,1)}, u32[]{:S(2)}, u32[]{:S(2)}) collective-permute-start(bf16[2,80,128,128]{3,1,2,0:T(8,128)(2,1)} %get-tuple-element.277), channel_id=1, source_target_pairs={{0,4},{4,8},{8,12},{12,16},{16,20},{20,24},{24,28},{28,0},{1,5},{5... | collective-permute-start | bytes 15728648 | tf_op jit(solution)/shard_map/while/body/eval_jaxpr/ppermute | solution.py:12
  837.5 4.7 slice-start.2
  837.5 5.9 slice-start.3
  841.9 8.7 slice-start
  843.4 7.1 slice-start.1
  850.5 7.4 copy-start.1
  858.0 8.7 copy-start
  866.7 112.8 %collective-permute-start = (bf16[2,80,128,128]{3,1,2,0:T(8,128)(2,1)}, bf16[2,80,128,128]{3,1,2,0:T(8,128)(2,1)}, u32[]{:S(2)}, u32[]{:S(2)}) collective-permute-start(bf16[2,80,128,128]{3,1,2,0:T(8,128)(2,1)} %get-tuple-element.277), channel_id=1, source_target_pairs={{0,4},{4,8},{8,12},{12,16},{16,20},{20,24},{24,28},{28,0},{1,5},{5... | collective-permute-start | bytes 15728648 | tf_op jit(solution)/shard_map/while/body/eval_jaxpr/ppermute | solution.py:12
  995.9 4.7 slice-start.2
  995.9 5.9 slice-start.3
  1000.3 8.7 slice-start
  1001.9 7.1 slice-start.1
  1008.9 7.4 copy-start.1
  1016.4 8.7 copy-start
  1025.1 111.9 %collective-permute-start = (bf16[2,80,128,128]{3,1,2,0:T(8,128)(2,1)}, bf16[2,80,128,128]{3,1,2,0:T(8,128)(2,1)}, u32[]{:S(2)}, u32[]{:S(2)}) collective-permute-start(bf16[2,80,128,128]{3,1,2,0:T(8,128)(2,1)} %get-tuple-element.277), channel_id=1, source_target_pairs={{0,4},{4,8},{8,12},{12,16},{16,20},{20,24},{24,28},{28,0},{1,5},{5... | collective-permute-start | bytes 15728648 | tf_op jit(solution)/shard_map/while/body/eval_jaxpr/ppermute | solution.py:12
  1153.4 4.7 slice-start.2
  1153.4 5.9 slice-start.3
  1157.8 8.6 slice-start
  1159.3 7.1 slice-start.1
  1166.4 7.4 copy-start.1
  1173.8 8.7 copy-start
Sparse Core Ops, SparseCore 0:
  8.9 36.9 all-gather.1
where the time goes:
time: 1210 us; the launch traced here: 1200 us
  waiting for transfers between devices  796 us (66%)
  local copies, waits for them, and re-layouts  186 us (15%)
  matrix products  179 us (15%)
  other arithmetic  21.6 us (2%)
  between operations  13.5 us (1%)
    ppermute x7, waiting for transfers between devices, passed_along(): return lax.ppermute(value, axis, pairs)  793 us
    while x91, local copies, waits for them, and re-layouts  72 us
    reshape x8, local copies, waits for them, and re-layouts, unpack_pair(): dense_cells.astype(jnp.bfloat16)  67 us
    dot_general x8, matrix products, unpack_pair(): jnp.einsum('st,gsde->gtde', chosen, buffer, preferred_element_type=jnp.fl...  61.3 us
    dot_general x8, matrix products, add_block(): jnp.dot(columns, gate_piece, preferred_element_type=jnp.float32)  59.7 us
    dot_general x8, matrix products, add_block(): jnp.dot(columns, up_piece, preferred_element_type=jnp.float32)  56.2 us
    slice x8, local copies, waits for them, and re-layouts, unpack_pair(): return (dense_cells[0], dense_cells[1])  34.6 us
  transfers between devices with their start and end apart: 8, of which 8 were waited for; matrix products, arithmetic and copies ran while one was open for 4% of the time, Pallas kernels for 0%

commit v1 on v0

v1 whole, which is shorter than its diff:
```python
import functools

import jax
import jax.numpy as jnp
from jax import lax
from jax.experimental import pallas as pl
from jax.experimental.pallas import tpu as pltpu
from jax.sharding import PartitionSpec as P

TILE = 128
VMEM_LIMIT = 56 * 1024 * 1024


def pack_kernel(row_tiles, col_tiles, core_ref, mask_ref, gate_ref, up_ref, mine_ref, other_ref):
    core = core_ref[0]

    def tile_step(i, j, slot):
        kept = mask_ref[i * col_tiles + j]
        rows = pl.ds(i * TILE, TILE)
        cols = pl.ds(pl.multiple_of(j * TILE, TILE), TILE)

        @pl.when((kept == 1) & (core == 0))
        def _():
            mine_ref[slot] = gate_ref[rows, cols]
            other_ref[slot] = up_ref[rows, cols]

        @pl.when((kept == 1) & (core == 1))
        def _():
            mine_ref[slot] = up_ref[rows, cols]
            other_ref[slot] = gate_ref[rows, cols]

        return slot + kept

    slot = jnp.int32(0)
    for i in range(row_tiles):
        slot = lax.fori_loop(0, col_tiles, functools.partial(tile_step, i), slot)


def block_kernel(row_tiles, col_tiles, chunk_tiles, first, last,
                 codes_ref, info_ref, tok_ref, mine_ref, other_ref, *rest):
    if first:
        acc_ref = None
        out_ref, dense = rest
    else:
        acc_ref, out_ref, dense = rest
    block, core = info_ref[0], info_ref[1]
    chunk = pl.program_id(0)
    sums = []
    for kind, packed in enumerate((mine_ref, other_ref)):
        for i in range(row_tiles):
            for j in range(chunk_tiles):
                code = codes_ref[(block * row_tiles + i) * col_tiles + chunk * chunk_tiles + j]
                tile = packed[jnp.maximum(code, 0)]
                dense[kind, pl.ds(i * TILE, TILE), pl.ds(j * TILE, TILE)] = jnp.where(
                    code >= 0, tile, jnp.zeros_like(tile))
        total = jnp.dot(tok_ref[...], dense[kind], preferred_element_type=jnp.float32)
        if not first:
            total = total + acc_ref[kind]
        if last:
            sums.append(total)
        else:
            out_ref[kind] = total
    if last:
        gate = jnp.where(core == 0, sums[0], sums[1])
        up = jnp.where(core == 0, sums[1], sums[0])
        out_ref[...] = (gate / (1.0 + jnp.exp(-gate)) * up).astype(out_ref.dtype)


def solution(mesh):
    R, C = mesh.shape["row"], mesh.shape["col"]
    NZ = R // 2
    axes = ("row", "col")

    def send(value, move):
        pairs = []
        for r in range(R):
            for c in range(C):
                tr, tc = move(r, c)
                pairs.append((r * C + c, tr * C + tc))
        return lax.ppermute(value, axes, pairs)

    sibling = lambda r, c: (r, c ^ 1)
    z_pair = lambda r, c: (r ^ 2, c)
    x_pair = lambda r, c: (r ^ 1, c)

    def swap_out(r, c):
        return (r, c) if ((r // 2) % 2) == (c % 2) else (r ^ 2, c ^ 1)

    def on_device(tokens, gate_weight, up_weight, tile_mask):
        depth, cols = gate_weight.shape
        row_tiles, col_tiles = depth // TILE, cols // TILE
        slots = 5 * row_tiles * col_tiles // 8
        rows = tokens.shape[0]
        r = lax.axis_index("row")
        core = lax.axis_index("col") % 2
        home = ((r // 2) % 2) == core

        smem = pl.BlockSpec(memory_space=pltpu.SMEM)
        vmem = pl.BlockSpec(memory_space=pltpu.VMEM)
        own_mask = lax.dynamic_slice_in_dim(tile_mask, r * row_tiles, row_tiles, 0).reshape(-1)
        piece = jax.ShapeDtypeStruct((slots, TILE, TILE), gate_weight.dtype)
        mine, other = pl.pallas_call(
            functools.partial(pack_kernel, row_tiles, col_tiles),
            out_shape=(piece, piece),
            in_specs=[smem, smem, vmem, vmem],
            out_specs=(vmem, vmem),
            compiler_params=pltpu.CompilerParams(vmem_limit_bytes=VMEM_LIMIT),
            name="pack",
        )(core.reshape(1).astype(jnp.int32), own_mask, gate_weight, up_weight)

        tok_other = send(tokens, z_pair)
        tok_mine = jnp.where(home, tokens, tok_other)
        tok_sib = send(jnp.where(home, tok_other, tokens), sibling)
        wide = tokens.shape[1]
        both = jnp.where(core == 0, jnp.concatenate([tok_mine, tok_sib], 1),
                         jnp.concatenate([tok_sib, tok_mine], 1))
        y = lax.axis_index("col") // 2
        tok = jnp.zeros((rows, wide * C), tokens.dtype)
        tok = lax.dynamic_update_slice_in_dim(tok, both, y * 2 * wide, 1)
        for s in range(1, C // 2):
            part = send(both, lambda rr, cc, s=s: (rr, (cc + 2 * s) % C))
            source = (y - s) % (C // 2)
            tok = lax.dynamic_update_slice_in_dim(tok, part, source * 2 * wide, 1)

        mask_sib = send(tile_mask, sibling)
        job_mask = jnp.where(home, tile_mask, mask_sib).reshape(R, row_tiles * col_tiles)
        place = jnp.arange(row_tiles * col_tiles)
        upto = (place[None, :] <= place[:, None]).astype(jnp.int32)
        slot = jnp.sum(job_mask[:, None, :] * upto[None], axis=2) - 1
        codes = jnp.where(job_mask == 1, slot, -1).reshape(-1)

        crossed = send(other, sibling)
        keep = jnp.where(home, mine, crossed)
        give = jnp.where(home, crossed, mine)
        own = [(keep, r), (send(give, z_pair), r ^ 2)]
        pieces = []
        for value, block in own:
            pieces.append((value, block))
            for s in range(1, NZ // 2):
                moved = send(value, lambda rr, cc, s=s: ((rr + 4 * s) % R, cc))
                pieces.append((moved, (block - 4 * s) % R))
        order = []
        for value, block in pieces:
            order.append((value, block))
            order.append((send(value, x_pair), block ^ 1))

        chunk_tiles = min(4, col_tiles)
        width = chunk_tiles * TILE
        acc = None
        for n, (value, block) in enumerate(order):
            across = send(value, sibling)
            first, last = n == 0, n == len(order) - 1
            info = jnp.stack([block, core]).astype(jnp.int32)
            whole = pl.BlockSpec((slots, TILE, TILE), lambda g, *_: (0, 0, 0))
            acc_spec = pl.BlockSpec((2, rows, width), lambda g, *_: (0, 0, g))
            in_specs = [pl.BlockSpec((rows, depth), lambda g, codes, info: (0, info[0])), whole, whole]
            operands = [codes, info, tok, value, across]
            if not first:
                in_specs.append(acc_spec)
                operands.append(acc)
            if last:
                out_shape = jax.ShapeDtypeStruct((rows, cols), jnp.bfloat16)
                out_spec = pl.BlockSpec((rows, width), lambda g, *_: (0, g))
            else:
                out_shape = jax.ShapeDtypeStruct((2, rows, cols), jnp.float32)
                out_spec = acc_spec
            acc = pl.pallas_call(
                functools.partial(block_kernel, row_tiles, col_tiles, chunk_tiles, first, last),
                out_shape=out_shape,
                grid_spec=pltpu.PrefetchScalarGridSpec(
                    num_scalar_prefetch=2,
                    grid=(cols // width,),
                    in_specs=in_specs,
                    out_specs=out_spec,
                    scratch_shapes=[pltpu.VMEM((2, depth, width), jnp.bfloat16)],
                ),
                input_output_aliases={} if first or last else {5: 0},
                compiler_params=pltpu.CompilerParams(vmem_limit_bytes=VMEM_LIMIT),
                cost_estimate=pl.CostEstimate(
                    flops=4 * rows * depth * cols,
                    bytes_accessed=8 * rows * cols * 2 + 4 * slots * TILE * TILE,
                    transcendentals=0),
                name="block",
            )(*operands)
        return send(acc, swap_out)

    placed = (P("row", "col"), P("row", "col"), P("row", "col"), P(None, "col"))
    return jax.shard_map(
        on_device, mesh=mesh, in_specs=placed, out_specs=P("row", "col"), check_vma=False
    )
```

time: 1210 us -> 523 us (0.43)
  waiting for transfers between devices: 796 us -> 316 us
  matrix products: 179 us -> 0 us
  local copies, waits for them, and re-layouts: 186 us -> 13.3 us
  Pallas kernels: 0 us -> 152 us
  starting transfers between devices: 1.23 us -> 24.6 us
  between operations: 13.5 us -> 0.07 us
    ppermute x7 -> x21, waiting for transfers between devices: 793 us -> 316 us  [send(): return lax.ppermute(value, axes, pairs)]
    dot_general x26 -> x0, matrix products: 179 us -> none  [the longest x8 61.3 us: unpack_pair(): jnp.einsum('st,gsde->gtde', chosen, buffer, preferred_element_type=jnp.fl...]
    pallas_call x0 -> x9, Pallas kernels: none -> 152 us  [the longest x8 143 us: on_device(): pl.pallas_call(functools.partial(block_kernel, row_tiles, col_tiles, chun...]
    while x91 -> x0, local copies, waits for them, and re-layouts: 72 us -> none
    reshape x8 -> x1, local copies, waits for them, and re-layouts: 67 us -> 0.56 us  [on_device(): lax.dynamic_slice_in_dim(tile_mask, r * row_tiles, row_tiles, 0).reshape(-1)]
    slice x8 -> x0, local copies, waits for them, and re-layouts: 34.6 us -> none  [unpack_pair(): return (dense_cells[0], dense_cells[1])]
    ppermute x7 -> x21, starting transfers between devices: 1.22 us -> 24.6 us  [send(): return lax.ppermute(value, axes, pairs)]
  transfers between devices with their start and end apart: 8 -> 21, of which waited for: 8 -> 8; matrix products, arithmetic and copies ran while one was open for 4% -> 4% of each run, Pallas kernels for 0% -> 24%
where the time goes in v1:
time: 523 us; the launch traced here: 522 us
  waiting for transfers between devices  316 us (60%)
  Pallas kernels  152 us (29%)
  starting transfers between devices  24.6 us (5%)
  other arithmetic  16.1 us (3%)
  local copies, waits for them, and re-layouts  13.3 us (3%)
    ppermute x21, waiting for transfers between devices, send(): return lax.ppermute(value, axes, pairs)  316 us
    pallas_call x8, Pallas kernels, on_device(): pl.pallas_call(functools.partial(block_kernel, row_tiles, col_tiles, chun...  143 us
    ppermute x21, starting transfers between devices, send(): return lax.ppermute(value, axes, pairs)  24.6 us
  transfers between devices with their start and end apart: 21, of which 8 were waited for; matrix products, arithmetic and copies ran while one was open for 4% of the time, Pallas kernels for 24%

profile of v1, /device:TPU:1, one launch (start us, length us, event | category | flops | bytes accessed | tf_op | source)
XLA Modules:
  0.0 522.1 jit_solution(11785205528123079604)
XLA Ops:
  0.0 0.7 constant_dynamic-slice_fusion
  0.7 0.6 reshape.26.mask_ref
  1.3 9.3 %pack.1 = (bf16[80,128,128]{2,1,0:T(8,128)(2,1)}, bf16[80,128,128]{2,1,0:T(8,128)(2,1)}) custom-call(s32[1]{0:T(128)} %bitcast.2.core_ref, s32[128]{0:T(128)} %reshape.26.mask_ref, bf16[512,4096]{1,0:T(8,128)(2,1)} %gate_ref.1, bf16[512,4096]{1,0:T(8,128)(2,1)} %up_ref.1), custom_call_target="tpu_custom_call" | custom-call | tf_op jit(solution)/shard_map/pack/pallas_call | solution.py:102
  10.5 0.2 collective-permute-start.4
  10.8 2.9 collective-permute-start.1
  13.7 1.9 collective-permute-done.4
  15.7 1.5 copy-done.5
  17.2 4.4 broadcast_select_fusion
  21.5 2.8 collective-permute-start.5
  24.3 2.2 collective-permute-start.13
  26.5 67.2 %collective-permute-done.1 = bf16[512,1024]{1,0:T(8,128)(2,1)} collective-permute-done((bf16[512,1024]{1,0:T(8,128)(2,1)}, bf16[512,1024]{1,0:T(8,128)(2,1)}, u32[]{:S(2)}, u32[]{:S(2)}) %collective-permute-start.1) | collective-permute-done | bytes 1048608 | tf_op jit(solution)/shard_map/ppermute | solution.py:80
  93.7 3.0 broadcast_select_fusion.2
  96.7 0.8 collective-permute-start.2
  97.5 1.4 collective-permute-start.17
  98.9 0.3 collective-permute-start
  99.2 1.0 collective-permute-done.2
  100.1 0.4 collective-permute-start.19
  100.5 2.5 broadcast_in_dim.3
  103.0 3.2 constant_dynamic-update-slice_fusion.1
  106.2 0.0 collective-permute-done
  106.2 1.6 collective-permute-start.3
  107.8 42.1 %collective-permute-done.5.mine_ref = bf16[80,128,128]{2,1,0:T(8,128)(2,1)} collective-permute-done((bf16[80,128,128]{2,1,0:T(8,128)(2,1)}, bf16[80,128,128]{2,1,0:T(8,128)(2,1)}, u32[]{:S(2)}, u32[]{:S(2)}) %collective-permute-start.5) | collective-permute-done | bytes 2621472 | tf_op jit(solution)/shard_map/ppermute | solution.py:80
  149.9 1.2 collective-permute-start.6
  151.1 1.3 collective-permute-start.14
  152.4 3.7 collective-permute-done.17.mine_ref
  156.1 1.2 collective-permute-start.18
  157.3 0.0 collective-permute-done.3
  157.3 1.4 collective-permute-start.10
  158.6 0.4 collective-permute-start.16
  159.0 1.1 copy-done.4
  160.1 105.1 %collective-permute-done.6.mine_ref = bf16[80,128,128]{2,1,0:T(8,128)(2,1)} collective-permute-done((bf16[80,128,128]{2,1,0:T(8,128)(2,1)}, bf16[80,128,128]{2,1,0:T(8,128)(2,1)}, u32[]{:S(2)}, u32[]{:S(2)}) %collective-permute-start.6) | collective-permute-done | bytes 2621472 | tf_op jit(solution)/shard_map/ppermute | solution.py:80
  265.3 0.6 collective-permute-start.7
  265.9 0.6 pad_add_fusion.7.info_ref
  266.5 0.6 pad_add_fusion.6.info_ref
  267.1 0.6 pad_add_fusion.5.info_ref
  267.6 1.9 collective-permute-start.15
  269.6 0.6 pad_add_fusion.4.info_ref
  270.2 0.6 pad_add_fusion.3.info_ref
  270.8 0.7 pad_add_fusion.2.info_ref
  271.4 0.6 pad_add_fusion.1.info_ref
  272.0 0.0 collective-permute-start.12
  272.0 0.6 pad_add_fusion.info_ref
  272.6 0.1 mul.26
  272.7 0.1 eq.21
  272.8 0.5 collective-permute-start.11
  273.3 0.2 multiply_reduce_fusion
  273.5 0.6 bitcast_select_fusion.codes_ref
  274.1 0.0 collective-permute-done.16.other_ref
  274.1 0.0 collective-permute-start.9
  274.1 3.2 constant_dynamic-update-slice_fusion.tok_ref
  277.3 46.4 %collective-permute-done.7.mine_ref = bf16[80,128,128]{2,1,0:T(8,128)(2,1)S(1)} collective-permute-done((bf16[80,128,128]{2,1,0:T(8,128)(2,1)}, bf16[80,128,128]{2,1,0:T(8,128)(2,1)S(1)}, u32[]{:S(2)}, u32[]{:S(2)}) %collective-permute-start.7) | collective-permute-done | bytes 2621472 | tf_op jit(solution)/shard_map/ppermute | solution.py:80
  323.6 1.7 collective-permute-start.8
  325.3 13.0 %block.8.rest_0_ = f32[2,512,4096]{2,1,0:T(8,128)} custom-call(s32[1024]{0:T(1024)} %bitcast_select_fusion.codes_ref, s32[2]{0:T(128)} %pad_add_fusion.7.info_ref, bf16[512,4096]{1,0:T(8,128)(2,1)} %constant_dynamic-update-slice_fusion.tok_ref, bf16[80,128,128]{2,1,0:T(8,128)(2,1)} %copy-done, bf16[80,128,128]{2,1,0:T(8,128)(2,1)} %copy-done.4), custom_call_target="tpu_custom_call" | custom-call | flops 4294967296 | bytes 38797312 | tf_op jit(solution)/shard_map/block/pallas_call | solution.py:167
  338.3 19.0 %block.9.rest_0_ = f32[2,512,4096]{2,1,0:T(8,128)} custom-call(s32[1024]{0:T(1024)} %bitcast_select_fusion.codes_ref, s32[2]{0:T(128)} %pad_add_fusion.6.info_ref, bf16[512,4096]{1,0:T(8,128)(2,1)} %constant_dynamic-update-slice_fusion.tok_ref, bf16[80,128,128]{2,1,0:T(8,128)(2,1)} %collective-permute-done.17.mine_ref, ...), custom_call_target="tpu_custom_call", output_to_operand_aliasing={{}: (5, {})} | custom-call | flops 4294967296 | bytes 38797312 | tf_op jit(solution)/shard_map/block/pallas_call | solution.py:167
  357.3 19.0 %block.10.rest_0_ = f32[2,512,4096]{2,1,0:T(8,128)} custom-call(s32[1024]{0:T(1024)} %bitcast_select_fusion.codes_ref, s32[2]{0:T(128)} %pad_add_fusion.5.info_ref, bf16[512,4096]{1,0:T(8,128)(2,1)} %constant_dynamic-update-slice_fusion.tok_ref, bf16[80,128,128]{2,1,0:T(8,128)(2,1)} %collective-permute-done.13.mine_ref, ...), custom_call_target="tpu_custom_call", output_to_operand_aliasing={{}: (5, {})} | custom-call | flops 4294967296 | bytes 38797312 | tf_op jit(solution)/shard_map/block/pallas_call | solution.py:167
  376.3 19.0 %block.11.rest_0_ = f32[2,512,4096]{2,1,0:T(8,128)} custom-call(s32[1024]{0:T(1024)} %bitcast_select_fusion.codes_ref, s32[2]{0:T(128)} %pad_add_fusion.4.info_ref, bf16[512,4096]{1,0:T(8,128)(2,1)} %constant_dynamic-update-slice_fusion.tok_ref, bf16[80,128,128]{2,1,0:T(8,128)(2,1)} %collective-permute-done.14.mine_ref, ...), custom_call_target="tpu_custom_call", output_to_operand_aliasing={{}: (5, {})} | custom-call | flops 4294967296 | bytes 38797312 | tf_op jit(solution)/shard_map/block/pallas_call | solution.py:167
  395.3 19.0 %block.12.rest_0_ = f32[2,512,4096]{2,1,0:T(8,128)} custom-call(s32[1024]{0:T(1024)} %bitcast_select_fusion.codes_ref, s32[2]{0:T(128)} %pad_add_fusion.3.info_ref, bf16[512,4096]{1,0:T(8,128)(2,1)} %constant_dynamic-update-slice_fusion.tok_ref, bf16[80,128,128]{2,1,0:T(8,128)(2,1)} %collective-permute-done.5.mine_ref, ...), custom_call_target="tpu_custom_call", output_to_operand_aliasing={{}: (5, {})} | custom-call | flops 4294967296 | bytes 38797312 | tf_op jit(solution)/shard_map/block/pallas_call | solution.py:167
  414.2 1.5 copy-done.3
  415.8 19.0 %block.13.rest_0_ = f32[2,512,4096]{2,1,0:T(8,128)} custom-call(s32[1024]{0:T(1024)} %bitcast_select_fusion.codes_ref, s32[2]{0:T(128)} %pad_add_fusion.2.info_ref, bf16[512,4096]{1,0:T(8,128)(2,1)} %constant_dynamic-update-slice_fusion.tok_ref, bf16[80,128,128]{2,1,0:T(8,128)(2,1)} %collective-permute-done.10.mine_ref, ...), custom_call_target="tpu_custom_call", output_to_operand_aliasing={{}: (5, {})} | custom-call | flops 4294967296 | bytes 38797312 | tf_op jit(solution)/shard_map/block/pallas_call | solution.py:167
  434.7 19.0 %block.14.rest_0_ = f32[2,512,4096]{2,1,0:T(8,128)} custom-call(s32[1024]{0:T(1024)} %bitcast_select_fusion.codes_ref, s32[2]{0:T(128)} %pad_add_fusion.1.info_ref, bf16[512,4096]{1,0:T(8,128)(2,1)} %constant_dynamic-update-slice_fusion.tok_ref, bf16[80,128,128]{2,1,0:T(8,128)(2,1)} %collective-permute-done.6.mine_ref, ...), custom_call_target="tpu_custom_call", output_to_operand_aliasing={{}: (5, {})} | custom-call | flops 4294967296 | bytes 38797312 | tf_op jit(solution)/shard_map/block/pallas_call | solution.py:167
  453.7 16.3 %block.15 = bf16[512,4096]{1,0:T(8,128)(2,1)} custom-call(s32[1024]{0:T(1024)} %bitcast_select_fusion.codes_ref, s32[2]{0:T(128)} %pad_add_fusion.info_ref, bf16[512,4096]{1,0:T(8,128)(2,1)} %constant_dynamic-update-slice_fusion.tok_ref, bf16[80,128,128]{2,1,0:T(8,128)(2,1)} %copy-done.2, bf16[80,128,128]{2,1,0:T(8,128)(2,1)} %collective-permute-done.8.other_ref, ...), custom_call_target="tpu_custom_call" | custom-call | flops 4294967296 | bytes 38797312 | tf_op jit(solution)/shard_map/block/pallas_call | solution.py:167
  470.1 1.9 collective-permute-start.20
  472.0 48.1 %collective-permute-done.20 = bf16[512,4096]{1,0:T(8,128)(2,1)S(1)} collective-permute-done((bf16[512,4096]{1,0:T(8,128)(2,1)}, bf16[512,4096]{1,0:T(8,128)(2,1)S(1)}, u32[]{:S(2)}, u32[]{:S(2)}) %collective-permute-start.20) | collective-permute-done | bytes 4194336 | tf_op jit(solution)/shard_map/ppermute | solution.py:80
  520.1 2.0 copy.20
  (25 shorter events, 0.1 us)
Async XLA Ops:
  10.5 5.1 collective-permute-start.4
  10.8 82.9 %collective-permute-start.1 = (bf16[512,1024]{1,0:T(8,128)(2,1)}, bf16[512,1024]{1,0:T(8,128)(2,1)}, u32[]{:S(2)}, u32[]{:S(2)}) collective-permute-start(bf16[512,1024]{1,0:T(8,128)(2,1)} %param.4), channel_id=1, source_target_pairs={{0,8},{1,9},{2,10},{3,11},{4,12},{5,13},{6,14},{7,15},{8,0},{9,1},... | collective-permute-start | bytes 3145736 | tf_op jit(solution)/shard_map/ppermute | solution.py:80
  15.7 1.5 copy-start.5
  21.5 81.5 %copy-start = (bf16[80,128,128]{2,1,0:T(8,128)(2,1)}, bf16[80,128,128]{2,1,0:T(8,128)(2,1)S(1)}, u32[]{:S(2)}) copy-start(bf16[80,128,128]{2,1,0:T(8,128)(2,1)S(1)} %get-tuple-element.13.mine_ref) | copy-start | bytes 7864324
  21.5 77.3 %copy-start.7 = (s32[32,32]{1,0:T(8,128)S(1)}, s32[32,32]{1,0:T(8,128)}, u32[]{:S(2)}) copy-start(s32[32,32]{1,0:T(8,128)} %param.7) | copy-start | bytes 12292
  21.5 128.4 %collective-permute-start.5 = (bf16[80,128,128]{2,1,0:T(8,128)(2,1)}, bf16[80,128,128]{2,1,0:T(8,128)(2,1)}, u32[]{:S(2)}, u32[]{:S(2)}) collective-permute-start(bf16[80,128,128]{2,1,0:T(8,128)(2,1)} %get-tuple-element.14), channel_id=1, source_target_pairs={{0,8},{1,9},{2,10},{3,11},{4,12},{5,13},{6,14},{7,15},{8,0},{9,1},... | collective-permute-start | bytes 7864328 | tf_op jit(solution)/shard_map/ppermute | solution.py:80
  24.3 126.8 %collective-permute-start.13 = (bf16[80,128,128]{2,1,0:T(8,128)(2,1)S(1)}, bf16[80,128,128]{2,1,0:T(8,128)(2,1)}, u32[]{:S(2)}, u32[]{:S(2)}) collective-permute-start(bf16[80,128,128]{2,1,0:T(8,128)(2,1)S(1)} %get-tuple-element.13.mine_ref), channel_id=1, source_target_pairs={{0,16},{1,17},{2,18},{3,19},{4,20},{5,21},{6,22},{7,23},{8,24},{9,... | collective-permute-start | bytes 7864328 | tf_op jit(solution)/shard_map/ppermute | solution.py:80
  96.7 3.4 collective-permute-start.2
  97.5 58.6 %collective-permute-start.17 = (bf16[80,128,128]{2,1,0:T(8,128)(2,1)S(1)}, bf16[80,128,128]{2,1,0:T(8,128)(2,1)}, u32[]{:S(2)}, u32[]{:S(2)}) collective-permute-start(bf16[80,128,128]{2,1,0:T(8,128)(2,1)S(1)} %get-tuple-element.13.mine_ref), channel_id=1, source_target_pairs={{0,4},{1,5},{2,6},{3,7},{4,0},{5,1},{6,2},{7,3},{8,12},{9,13},{10,... | collective-permute-start | bytes 7864328 | tf_op jit(solution)/shard_map/ppermute | solution.py:80
  98.9 7.4 %collective-permute-start = (s32[32,32]{1,0:T(8,128)S(1)}, s32[32,32]{1,0:T(8,128)S(1)}, u32[]{:S(2)}, u32[]{:S(2)}) collective-permute-start(s32[32,32]{1,0:T(8,128)S(1)} %copy-done.7), channel_id=1, source_target_pairs={{0,1},{1,0},{2,3},{3,2},{4,5},{5,4},{6,7},{7,6},{8,9},{9,8},{10,11... | collective-permute-start | bytes 12296 | tf_op jit(solution)/shard_map/ppermute | solution.py:80
  99.2 3.9 copy-start.1
  100.1 58.5 %collective-permute-start.19 = (bf16[80,128,128]{2,1,0:T(8,128)(2,1)S(1)}, bf16[80,128,128]{2,1,0:T(8,128)(2,1)S(1)}, u32[]{:S(2)}, u32[]{:S(2)}) collective-permute-start(bf16[80,128,128]{2,1,0:T(8,128)(2,1)S(1)} %get-tuple-element.13.mine_ref), channel_id=1, source_target_pairs={{0,1},{1,0},{2,3},{3,2},{4,5},{5,4},{6,7},{7,6},{8,9},{9,8},{10,11... | collective-permute-start | bytes 7864328 | tf_op jit(solution)/shard_map/ppermute | solution.py:80
  106.2 51.0 %collective-permute-start.3 = (bf16[512,2048]{1,0:T(8,128)(2,1)S(1)}, bf16[512,2048]{1,0:T(8,128)(2,1)S(1)}, u32[]{:S(2)}, u32[]{:S(2)}) collective-permute-start(bf16[512,2048]{1,0:T(8,128)(2,1)S(1)} %get-tuple-element.10), channel_id=1, source_target_pairs={{0,2},{1,3},{2,0},{3,1},{4,6},{5,7},{6,4},{7,5},{8,10},{9,11},{10,... | collective-permute-start | bytes 6291464 | tf_op jit(solution)/shard_map/ppermute | solution.py:80
  149.9 115.4 %collective-permute-start.6 = (bf16[80,128,128]{2,1,0:T(8,128)(2,1)}, bf16[80,128,128]{2,1,0:T(8,128)(2,1)}, u32[]{:S(2)}, u32[]{:S(2)}) collective-permute-start(bf16[80,128,128]{2,1,0:T(8,128)(2,1)} %collective-permute-done.5.mine_ref), channel_id=1, source_target_pairs={{0,16},{1,17},{2,18},{3,19},{4,20},{5,21},{6,22},{7,23},{8,24},{9,... | collective-permute-start | bytes 7864328 | tf_op jit(solution)/shard_map/ppermute | solution.py:80
  151.1 116.5 %collective-permute-start.14 = (bf16[80,128,128]{2,1,0:T(8,128)(2,1)}, bf16[80,128,128]{2,1,0:T(8,128)(2,1)}, u32[]{:S(2)}, u32[]{:S(2)}) collective-permute-start(bf16[80,128,128]{2,1,0:T(8,128)(2,1)} %collective-permute-done.13.mine_ref), channel_id=1, source_target_pairs={{0,4},{1,5},{2,6},{3,7},{4,0},{5,1},{6,2},{7,3},{8,12},{9,13},{10,... | collective-permute-start | bytes 7864328 | tf_op jit(solution)/shard_map/ppermute | solution.py:80
  156.1 115.9 %collective-permute-start.18 = (bf16[80,128,128]{2,1,0:T(8,128)(2,1)}, bf16[80,128,128]{2,1,0:T(8,128)(2,1)}, u32[]{:S(2)}, u32[]{:S(2)}) collective-permute-start(bf16[80,128,128]{2,1,0:T(8,128)(2,1)} %collective-permute-done.17.mine_ref), channel_id=1, source_target_pairs={{0,1},{1,0},{2,3},{3,2},{4,5},{5,4},{6,7},{7,6},{8,9},{9,8},{10,11... | collective-permute-start | bytes 7864328 | tf_op jit(solution)/shard_map/ppermute | solution.py:80
  157.3 108.0 %copy-start.6 = (bf16[512,2048]{1,0:T(8,128)(2,1)}, bf16[512,2048]{1,0:T(8,128)(2,1)S(1)}, u32[]{:S(2)}) copy-start(bf16[512,2048]{1,0:T(8,128)(2,1)S(1)} %collective-permute-done.3) | copy-start | bytes 6291460
  157.3 115.5 %collective-permute-start.10 = (bf16[80,128,128]{2,1,0:T(8,128)(2,1)}, bf16[80,128,128]{2,1,0:T(8,128)(2,1)}, u32[]{:S(2)}, u32[]{:S(2)}) collective-permute-start(bf16[80,128,128]{2,1,0:T(8,128)(2,1)} %collective-permute-done.5.mine_ref), channel_id=1, source_target_pairs={{0,4},{1,5},{2,6},{3,7},{4,0},{5,1},{6,2},{7,3},{8,12},{9,13},{10,... | collective-permute-start | bytes 7864328 | tf_op jit(solution)/shard_map/ppermute | solution.py:80
  158.6 1.5 copy-start.4
  158.6 115.4 %collective-permute-start.16 = (bf16[80,128,128]{2,1,0:T(8,128)(2,1)}, bf16[80,128,128]{2,1,0:T(8,128)(2,1)}, u32[]{:S(2)}, u32[]{:S(2)}) collective-permute-start(bf16[80,128,128]{2,1,0:T(8,128)(2,1)} %collective-permute-done.13.mine_ref), channel_id=1, source_target_pairs={{0,1},{1,0},{2,3},{3,2},{4,5},{5,4},{6,7},{7,6},{8,9},{9,8},{10,11... | collective-permute-start | bytes 7864328 | tf_op jit(solution)/shard_map/ppermute | solution.py:80
  265.3 58.4 %collective-permute-start.7 = (bf16[80,128,128]{2,1,0:T(8,128)(2,1)}, bf16[80,128,128]{2,1,0:T(8,128)(2,1)S(1)}, u32[]{:S(2)}, u32[]{:S(2)}) collective-permute-start(bf16[80,128,128]{2,1,0:T(8,128)(2,1)} %collective-permute-done.6.mine_ref), channel_id=1, source_target_pairs={{0,4},{1,5},{2,6},{3,7},{4,0},{5,1},{6,2},{7,3},{8,12},{9,13},{10,... | collective-permute-start | bytes 7864328 | tf_op jit(solution)/shard_map/ppermute | solution.py:80
  267.6 108.6 %collective-permute-start.15 = (bf16[80,128,128]{2,1,0:T(8,128)(2,1)}, bf16[80,128,128]{2,1,0:T(8,128)(2,1)}, u32[]{:S(2)}, u32[]{:S(2)}) collective-permute-start(bf16[80,128,128]{2,1,0:T(8,128)(2,1)} %collective-permute-done.14.mine_ref), channel_id=1, source_target_pairs={{0,1},{1,0},{2,3},{3,2},{4,5},{5,4},{6,7},{7,6},{8,9},{9,8},{10,11... | collective-permute-start | bytes 7864328 | tf_op jit(solution)/shard_map/ppermute | solution.py:80
  272.0 123.3 %collective-permute-start.12 = (bf16[80,128,128]{2,1,0:T(8,128)(2,1)}, bf16[80,128,128]{2,1,0:T(8,128)(2,1)}, u32[]{:S(2)}, u32[]{:S(2)}) collective-permute-start(bf16[80,128,128]{2,1,0:T(8,128)(2,1)} %collective-permute-done.5.mine_ref), channel_id=1, source_target_pairs={{0,1},{1,0},{2,3},{3,2},{4,5},{5,4},{6,7},{7,6},{8,9},{9,8},{10,11... | collective-permute-start | bytes 7864328 | tf_op jit(solution)/shard_map/ppermute | solution.py:80
  272.8 141.5 %collective-permute-start.11 = (bf16[80,128,128]{2,1,0:T(8,128)(2,1)}, bf16[80,128,128]{2,1,0:T(8,128)(2,1)S(1)}, u32[]{:S(2)}, u32[]{:S(2)}) collective-permute-start(bf16[80,128,128]{2,1,0:T(8,128)(2,1)} %collective-permute-done.10.mine_ref), channel_id=1, source_target_pairs={{0,1},{1,0},{2,3},{3,2},{4,5},{5,4},{6,7},{7,6},{8,9},{9,8},{10,11... | collective-permute-start | bytes 7864328 | tf_op jit(solution)/shard_map/ppermute | solution.py:80
  274.1 160.7 %collective-permute-start.9 = (bf16[80,128,128]{2,1,0:T(8,128)(2,1)}, bf16[80,128,128]{2,1,0:T(8,128)(2,1)}, u32[]{:S(2)}, u32[]{:S(2)}) collective-permute-start(bf16[80,128,128]{2,1,0:T(8,128)(2,1)} %collective-permute-done.6.mine_ref), channel_id=1, source_target_pairs={{0,1},{1,0},{2,3},{3,2},{4,5},{5,4},{6,7},{7,6},{8,9},{9,8},{10,11... | collective-permute-start | bytes 7864328 | tf_op jit(solution)/shard_map/ppermute | solution.py:80
  323.6 14.7 %copy-start.2 = (bf16[80,128,128]{2,1,0:T(8,128)(2,1)}, bf16[80,128,128]{2,1,0:T(8,128)(2,1)S(1)}, u32[]{:S(2)}) copy-start(bf16[80,128,128]{2,1,0:T(8,128)(2,1)S(1)} %collective-permute-done.7.mine_ref) | copy-start | bytes 7864324
  323.6 130.1 %collective-permute-start.8 = (bf16[80,128,128]{2,1,0:T(8,128)(2,1)S(1)}, bf16[80,128,128]{2,1,0:T(8,128)(2,1)}, u32[]{:S(2)}, u32[]{:S(2)}) collective-permute-start(bf16[80,128,128]{2,1,0:T(8,128)(2,1)S(1)} %collective-permute-done.7.mine_ref), channel_id=1, source_target_pairs={{0,1},{1,0},{2,3},{3,2},{4,5},{5,4},{6,7},{7,6},{8,9},{9,8},{10,11... | collective-permute-start | bytes 7864328 | tf_op jit(solution)/shard_map/ppermute | solution.py:80
  414.2 1.5 copy-start.3
  470.1 50.0 %collective-permute-start.20 = (bf16[512,4096]{1,0:T(8,128)(2,1)}, bf16[512,4096]{1,0:T(8,128)(2,1)S(1)}, u32[]{:S(2)}, u32[]{:S(2)}) collective-permute-start(bf16[512,4096]{1,0:T(8,128)(2,1)} %block.15), channel_id=1, source_target_pairs={{0,0},{1,8},{2,2},{3,10},{4,4},{5,12},{6,6},{7,14},{8,1},{9,9},{10... | collective-permute-start | bytes 12582920 | tf_op jit(solution)/shard_map/ppermute | solution.py:80

commit v2 on v1

v2 whole, which is shorter than its diff:
```python
import functools

import jax
import jax.numpy as jnp
from jax import lax
from jax.experimental import pallas as pl
from jax.experimental.pallas import tpu as pltpu
from jax.sharding import PartitionSpec as P

TILE = 128
VMEM_LIMIT = 56 * 1024 * 1024


def pack_kernel(row_tiles, col_tiles, core_ref, mask_ref, gate_ref, up_ref, mine_ref, other_ref):
    core = core_ref[0]

    def tile_step(i, j, slot):
        kept = mask_ref[i * col_tiles + j]
        rows = pl.ds(i * TILE, TILE)
        cols = pl.ds(pl.multiple_of(j * TILE, TILE), TILE)

        @pl.when((kept == 1) & (core == 0))
        def _():
            mine_ref[slot] = gate_ref[rows, cols]
            other_ref[slot] = up_ref[rows, cols]

        @pl.when((kept == 1) & (core == 1))
        def _():
            mine_ref[slot] = up_ref[rows, cols]
            other_ref[slot] = gate_ref[rows, cols]

        return slot + kept

    slot = jnp.int32(0)
    for i in range(row_tiles):
        slot = lax.fori_loop(0, col_tiles, functools.partial(tile_step, i), slot)


def block_kernel(row_tiles, col_tiles, chunk_tiles, parts, first, last,
                 codes_ref, info_ref, tok_ref, *rest):
    pieces, rest = rest[:2 * parts], rest[2 * parts:]
    if first:
        acc_ref = None
    else:
        acc_ref, rest = rest[0], rest[1:]
    out_ref, packed, dense, sems = rest
    block, core = info_ref[0], info_ref[1]
    chunk = pl.program_id(0)

    @pl.when(chunk == 0)
    def _():
        copies = []
        for kind in range(2):
            start = 0
            for n in range(parts):
                ref = pieces[kind * parts + n]
                count = ref.shape[0]
                copies.append(pltpu.make_async_copy(
                    ref, packed.at[kind, pl.ds(start, count)], sems.at[kind, n]))
                start += count
        for copy in copies:
            copy.start()
        for copy in copies:
            copy.wait()

    sums = []
    for kind in range(2):
        for i in range(row_tiles):
            for j in range(chunk_tiles):
                code = codes_ref[(block * row_tiles + i) * col_tiles + chunk * chunk_tiles + j]
                tile = packed[kind, jnp.maximum(code, 0)]
                dense[kind, pl.ds(i * TILE, TILE), pl.ds(j * TILE, TILE)] = jnp.where(
                    code >= 0, tile, jnp.zeros_like(tile))
        total = jnp.dot(tok_ref[...], dense[kind], preferred_element_type=jnp.float32)
        if not first:
            total = total + acc_ref[kind]
        if last:
            sums.append(total)
        else:
            out_ref[kind] = total
    if last:
        gate = jnp.where(core == 0, sums[0], sums[1])
        up = jnp.where(core == 0, sums[1], sums[0])
        out_ref[...] = (gate / (1.0 + jnp.exp(-gate)) * up).astype(out_ref.dtype)


def solution(mesh):
    R, C = mesh.shape["row"], mesh.shape["col"]
    NZ = R // 2
    axes = ("row", "col")

    def send(value, move):
        pairs = []
        for r in range(R):
            for c in range(C):
                tr, tc = move(r, c)
                pairs.append((r * C + c, tr * C + tc))
        return lax.ppermute(value, axes, pairs)

    sibling = lambda r, c: (r, c ^ 1)
    z_pair = lambda r, c: (r ^ 2, c)
    x_pair = lambda r, c: (r ^ 1, c)

    def swap_out(r, c):
        return (r, c) if ((r // 2) % 2) == (c % 2) else (r ^ 2, c ^ 1)

    def on_device(tokens, gate_weight, up_weight, tile_mask):
        depth, cols = gate_weight.shape
        row_tiles, col_tiles = depth // TILE, cols // TILE
        slots = 5 * row_tiles * col_tiles // 8
        rows = tokens.shape[0]
        r = lax.axis_index("row")
        core = lax.axis_index("col") % 2
        home = ((r // 2) % 2) == core

        smem = pl.BlockSpec(memory_space=pltpu.SMEM)
        vmem = pl.BlockSpec(memory_space=pltpu.VMEM)
        own_mask = lax.dynamic_slice_in_dim(tile_mask, r * row_tiles, row_tiles, 0).reshape(-1)
        piece = jax.ShapeDtypeStruct((slots, TILE, TILE), gate_weight.dtype)
        mine, other = pl.pallas_call(
            functools.partial(pack_kernel, row_tiles, col_tiles),
            out_shape=(piece, piece),
            in_specs=[smem, smem, vmem, vmem],
            out_specs=(vmem, vmem),
            compiler_params=pltpu.CompilerParams(vmem_limit_bytes=VMEM_LIMIT),
            name="pack",
        )(core.reshape(1).astype(jnp.int32), own_mask, gate_weight, up_weight)

        mask_sib = send(tile_mask, sibling)
        job_mask = jnp.where(home, tile_mask, mask_sib).reshape(R, row_tiles * col_tiles)
        place = jnp.arange(row_tiles * col_tiles)
        upto = (place[None, :] <= place[:, None]).astype(jnp.int32)
        slot = jnp.sum(job_mask[:, None, :] * upto[None], axis=2) - 1
        codes = jnp.where(job_mask == 1, slot, -1).reshape(-1)

        crossed = send(other, sibling)
        keep = jnp.where(home, mine, crossed)
        give = jnp.where(home, crossed, mine)
        chunk_tiles = min(4, col_tiles)
        width = chunk_tiles * TILE

        def add_block(acc, values, block, last=False):
            first, parts = acc is None, len(values)
            info = jnp.stack([block, core]).astype(jnp.int32)
            acc_spec = pl.BlockSpec((2, rows, width), lambda g, *_: (0, 0, g))
            in_specs = [pl.BlockSpec((rows, depth), lambda g, codes, info: (0, info[0]))]
            in_specs += [pl.BlockSpec(memory_space=pl.ANY)] * (2 * parts)
            operands = [codes, info, tok] + [v for v, _ in values] + [w for _, w in values]
            if not first:
                in_specs.append(acc_spec)
                operands.append(acc)
            if last:
                out_shape = jax.ShapeDtypeStruct((rows, cols), jnp.bfloat16)
                out_spec = pl.BlockSpec((rows, width), lambda g, *_: (0, g))
            else:
                out_shape = jax.ShapeDtypeStruct((2, rows, cols), jnp.float32)
                out_spec = acc_spec
            return pl.pallas_call(
                functools.partial(block_kernel, row_tiles, col_tiles, chunk_tiles, parts, first, last),
                out_shape=out_shape,
                grid_spec=pltpu.PrefetchScalarGridSpec(
                    num_scalar_prefetch=2,
                    grid=(cols // width,),
                    in_specs=in_specs,
                    out_specs=out_spec,
                    scratch_shapes=[pltpu.VMEM((2, slots, TILE, TILE), jnp.bfloat16),
                                    pltpu.VMEM((2, depth, width), jnp.bfloat16),
                                    pltpu.SemaphoreType.DMA((2, parts))],
                ),
                input_output_aliases={} if first or last else {len(operands) - 1: 0},
                compiler_params=pltpu.CompilerParams(vmem_limit_bytes=VMEM_LIMIT),
                cost_estimate=pl.CostEstimate(
                    flops=rows * depth,
                    bytes_accessed=rows * depth,
                    transcendentals=0),
                name="block",
            )(*operands)

        def after(value, acc):
            return lax.optimization_barrier((value, acc))

        def along(value, s):
            return send(value, lambda rr, cc: ((rr + 4 * s) % R, cc))

        def with_sibling(value):
            return (value, send(value, sibling))

        paired = send(give, z_pair)
        far = [along(keep, s) for s in range(1, NZ // 2)]
        keep_x = send(keep, x_pair)
        tok_other = send(tokens, z_pair)
        half = slots // 2
        far, paired = after(far, paired)
        far_paired = [along(paired, s) for s in range(1, NZ // 2)]
        far_x = [send(value, x_pair) for value in far]
        paired_x = send(paired, x_pair)
        tok_other, (far, keep_x) = after(tok_other, (far, keep_x))
        tok_mine = jnp.where(home, tokens, tok_other)
        tok_sib = send(jnp.where(home, tok_other, tokens), sibling)
        wide = tokens.shape[1]
        both = jnp.where(core == 0, jnp.concatenate([tok_mine, tok_sib], 1),
                         jnp.concatenate([tok_sib, tok_mine], 1))
        y = lax.axis_index("col") // 2
        tok = jnp.zeros((rows, wide * C), tokens.dtype)
        tok = lax.dynamic_update_slice_in_dim(tok, both, y * 2 * wide, 1)
        for s in range(1, C // 2):
            part = send(both, lambda rr, cc, s=s: (rr, (cc + 2 * s) % C))
            source = (y - s) % (C // 2)
            tok = lax.dynamic_update_slice_in_dim(tok, part, source * 2 * wide, 1)

        acc = add_block(None, [with_sibling(keep)], r)
        acc = add_block(acc, [with_sibling(keep_x)], r ^ 1)
        acc = add_block(acc, [with_sibling(paired)], r ^ 2)
        for s, value in enumerate(far, 1):
            acc = add_block(acc, [with_sibling(value)], (r - 4 * s) % R)
        far_paired, acc = after(far_paired, acc)
        (far_x, paired_x), far_paired = after((far_x, paired_x), far_paired)
        last_a = [send(value[:half], x_pair) for value in far_paired]
        last_b = [along(paired_x[half:], s) for s in range(1, NZ // 2)]
        for s, value in enumerate(far_x, 1):
            acc = add_block(acc, [with_sibling(value)], ((r - 4 * s) % R) ^ 1)
        acc = add_block(acc, [with_sibling(paired_x)], r ^ 3)
        for s, value in enumerate(far_paired, 1):
            acc = add_block(acc, [with_sibling(value)], ((r ^ 2) - 4 * s) % R)
        (last_a, last_b), acc = after((last_a, last_b), acc)
        for s in range(1, NZ // 2):
            acc = add_block(acc, [with_sibling(last_a[s - 1]), with_sibling(last_b[s - 1])],
                            (((r ^ 2) - 4 * s) % R) ^ 1, last=s == NZ // 2 - 1)
        return send(acc, swap_out)

    placed = (P("row", "col"), P("row", "col"), P("row", "col"), P(None, "col"))
    return jax.shard_map(
        on_device, mesh=mesh, in_specs=placed, out_specs=P("row", "col"), check_vma=False
    )
```

time: 523 us -> 447 us (0.85)
  waiting for transfers between devices: 316 us -> 234 us
  Pallas kernels: 152 us -> 161 us
    ppermute x21 -> x23, waiting for transfers between devices: 316 us -> 234 us  [send(): return lax.ppermute(value, axes, pairs)]
    pallas_call x8, Pallas kernels: 143 us -> 151 us  [add_block(): pl.pallas_call(functools.partial(block_kernel, row_tiles, col_tiles, chun...]
    ppermute x21 -> x23, starting transfers between devices: 24.6 us -> 21.8 us  [send(): return lax.ppermute(value, axes, pairs)]
  transfers between devices with their start and end apart: 21 -> 23, of which waited for: 8 -> 9; matrix products, arithmetic and copies ran while one was open for 4% -> 4% of each run, Pallas kernels for 24% -> 30%
where the time goes in v2:
time: 447 us; the launch traced here: 446 us
  waiting for transfers between devices  234 us (52%)
  Pallas kernels  161 us (36%)
  starting transfers between devices  21.8 us (5%)
  local copies, waits for them, and re-layouts  15.6 us (3%)
  other arithmetic  13.4 us (3%)
    ppermute x23, waiting for transfers between devices, send(): return lax.ppermute(value, axes, pairs)  234 us
    pallas_call x8, Pallas kernels, add_block(): pl.pallas_call(functools.partial(block_kernel, row_tiles, col_tiles, chun...  151 us
    ppermute x23, starting transfers between devices, send(): return lax.ppermute(value, axes, pairs)  21.8 us
    pallas_call x1, Pallas kernels, on_device(): pl.pallas_call(functools.partial(pack_kernel, row_tiles, col_tiles), out_...  9.62 us
  transfers between devices with their start and end apart: 23, of which 9 were waited for; matrix products, arithmetic and copies ran while one was open for 4% of the time, Pallas kernels for 30%

profile of v2, /device:TPU:1, one launch (start us, length us, event | category | flops | bytes accessed | tf_op | source)
XLA Modules:
  0.0 446.1 jit_solution(13632546200057516209)
XLA Ops:
  0.0 0.7 constant_dynamic-slice_fusion
  0.7 0.7 reshape.26.mask_ref
  1.4 9.6 %pack.1 = (bf16[80,128,128]{2,1,0:T(8,128)(2,1)}, bf16[80,128,128]{2,1,0:T(8,128)(2,1)}) custom-call(s32[1]{0:T(128)} %bitcast.2.core_ref, s32[128]{0:T(128)} %reshape.26.mask_ref, bf16[512,4096]{1,0:T(8,128)(2,1)} %gate_ref.1, bf16[512,4096]{1,0:T(8,128)(2,1)} %up_ref.1), custom_call_target="tpu_custom_call" | custom-call | tf_op jit(solution)/shard_map/pack/pallas_call | solution.py:120
  11.0 0.0 collective-permute-start.2
  11.0 5.1 %collective-permute-done.2 = bf16[80,128,128]{2,1,0:T(8,128)(2,1)S(1)} collective-permute-done((bf16[80,128,128]{2,1,0:T(8,128)(2,1)}, bf16[80,128,128]{2,1,0:T(8,128)(2,1)S(1)}, u32[]{:S(2)}, u32[]{:S(2)}) %collective-permute-start.2) | collective-permute-done | bytes 2621472 | tf_op jit(solution)/shard_map/ppermute | solution.py:98
  16.1 1.5 copy-done.3
  17.6 3.0 broadcast_select_fusion
  20.6 3.3 collective-permute-start.3
  23.9 1.3 collective-permute-start.4
  25.2 1.2 collective-permute-start.5
  26.4 0.1 collective-permute-start.1
  26.5 110.7 %collective-permute-done.3.rest_0_ = bf16[80,128,128]{2,1,0:T(8,128)(2,1)} collective-permute-done((bf16[80,128,128]{2,1,0:T(8,128)(2,1)S(1)}, bf16[80,128,128]{2,1,0:T(8,128)(2,1)}, u32[]{:S(2)}, u32[]{:S(2)}) %collective-permute-start.3) | collective-permute-done | bytes 2621472 | tf_op jit(solution)/shard_map/ppermute | solution.py:98
  137.2 0.0 collective-permute-done.4.rest_0_
  137.2 21.9 %collective-permute-done.1 = bf16[512,1024]{1,0:T(8,128)(2,1)S(1)} collective-permute-done((bf16[512,1024]{1,0:T(8,128)(2,1)S(1)}, bf16[512,1024]{1,0:T(8,128)(2,1)S(1)}, u32[]{:S(2)}, u32[]{:S(2)}) %collective-permute-start.1) | collective-permute-done | bytes 1048608 | tf_op jit(solution)/shard_map/ppermute | solution.py:98
  159.1 1.5 broadcast_select_fusion.2
  160.6 1.5 collective-permute-start.6
  162.1 0.5 collective-permute-start.13
  162.6 3.6 collective-permute-done.6
  166.2 2.5 broadcast_in_dim.3
  168.7 3.3 constant_dynamic-update-slice_fusion.1
  172.0 1.4 collective-permute-start.7
  173.4 0.7 collective-permute-start
  174.0 0.0 collective-permute-start.12
  174.1 0.8 collective-permute-done
  174.9 0.3 collective-permute-start.11
  175.2 1.0 collective-permute-start.10
  176.2 1.1 collective-permute-start.8
  177.4 41.5 %collective-permute-done.7 = bf16[512,2048]{1,0:T(8,128)(2,1)} collective-permute-done((bf16[512,2048]{1,0:T(8,128)(2,1)S(1)}, bf16[512,2048]{1,0:T(8,128)(2,1)}, u32[]{:S(2)}, u32[]{:S(2)}) %collective-permute-start.7) | collective-permute-done | bytes 2097184 | tf_op jit(solution)/shard_map/ppermute | solution.py:98
  218.9 1.7 collective-permute-start.9
  220.6 0.6 pad_add_fusion.4.info_ref
  221.2 0.6 pad_add_fusion.3.info_ref
  221.8 0.6 pad_add_fusion.2.info_ref
  222.4 0.1 mul.26
  222.5 0.1 eq.23
  222.6 0.2 multiply_reduce_fusion
  222.8 0.6 bitcast_select_fusion.codes_ref
  223.4 3.2 constant_dynamic-update-slice_fusion.tok_ref
  226.5 13.8 %block.8.rest_2_ = f32[2,512,4096]{2,1,0:T(8,128)} custom-call(s32[1024]{0:T(1024)} %bitcast_select_fusion.codes_ref, s32[2]{0:T(128)} %pad_add_fusion.4.info_ref, bf16[512,4096]{1,0:T(8,128)(2,1)} %constant_dynamic-update-slice_fusion.tok_ref, bf16[80,128,128]{2,1,0:T(8,128)(2,1)} %copy-done, bf16[80,128,128]{2,1,0:T(8,128)(2,1)} %collective-permute-done.14.rest_1_), custom_call_target="tpu_custom_call" | custom-call | flops 262144 | bytes 262144 | tf_op jit(solution)/shard_map/block/pallas_call | solution.py:158
  240.4 0.6 pad_add_fusion.1.info_ref
  241.0 20.0 %block.9.rest_2_ = f32[2,512,4096]{2,1,0:T(8,128)} custom-call(s32[1024]{0:T(1024)} %bitcast_select_fusion.codes_ref, s32[2]{0:T(128)} %pad_add_fusion.3.info_ref, bf16[512,4096]{1,0:T(8,128)(2,1)} %constant_dynamic-update-slice_fusion.tok_ref, bf16[80,128,128]{2,1,0:T(8,128)(2,1)} %collective-permute-done.5.rest_0_, ...), custom_call_target="tpu_custom_call", output_to_operand_aliasing={{}: (5, {})} | custom-call | flops 262144 | bytes 262144 | tf_op jit(solution)/shard_map/block/pallas_call | solution.py:158
  261.0 20.0 %block.10.rest_2_ = f32[2,512,4096]{2,1,0:T(8,128)} custom-call(s32[1024]{0:T(1024)} %bitcast_select_fusion.codes_ref, s32[2]{0:T(128)} %pad_add_fusion.2.info_ref, bf16[512,4096]{1,0:T(8,128)(2,1)} %constant_dynamic-update-slice_fusion.tok_ref, bf16[80,128,128]{2,1,0:T(8,128)(2,1)} %collective-permute-done.4.rest_0_, ...), custom_call_target="tpu_custom_call", output_to_operand_aliasing={{}: (5, {})} | custom-call | flops 262144 | bytes 262144 | tf_op jit(solution)/shard_map/block/pallas_call | solution.py:158
  281.0 20.0 %block.11.rest_2_ = f32[2,512,4096]{2,1,0:T(8,128)} custom-call(s32[1024]{0:T(1024)} %bitcast_select_fusion.codes_ref, s32[2]{0:T(128)} %pad_add_fusion.1.info_ref, bf16[512,4096]{1,0:T(8,128)(2,1)} %constant_dynamic-update-slice_fusion.tok_ref, bf16[80,128,128]{2,1,0:T(8,128)(2,1)} %collective-permute-done.3.rest_0_, ...), custom_call_target="tpu_custom_call", output_to_operand_aliasing={{}: (5, {})} | custom-call | flops 262144 | bytes 262144 | tf_op jit(solution)/shard_map/block/pallas_call | solution.py:158
  301.1 1.4 collective-permute-start.19
  302.5 0.1 collective-permute-start.18
  302.6 0.4 collective-permute-start.17
  303.0 1.1 slice.6
  304.1 2.6 slice.7
  306.7 1.2 collective-permute-start.16
  307.9 0.6 pad_add_fusion.7.info_ref
  308.6 0.6 pad_add_fusion.6.info_ref
  309.2 0.7 pad_add_fusion.5.info_ref
  309.8 20.0 %block.12.rest_2_ = f32[2,512,4096]{2,1,0:T(8,128)} custom-call(s32[1024]{0:T(1024)} %bitcast_select_fusion.codes_ref, s32[2]{0:T(128)} %pad_add_fusion.7.info_ref, bf16[512,4096]{1,0:T(8,128)(2,1)} %constant_dynamic-update-slice_fusion.tok_ref, bf16[80,128,128]{2,1,0:T(8,128)(2,1)} %collective-permute-done.8.rest_0_, ...), custom_call_target="tpu_custom_call", output_to_operand_aliasing={{}: (5, {})} | custom-call | flops 262144 | bytes 262144 | tf_op jit(solution)/shard_map/block/pallas_call | solution.py:158
  329.9 20.0 %block.13.rest_2_ = f32[2,512,4096]{2,1,0:T(8,128)} custom-call(s32[1024]{0:T(1024)} %bitcast_select_fusion.codes_ref, s32[2]{0:T(128)} %pad_add_fusion.6.info_ref, bf16[512,4096]{1,0:T(8,128)(2,1)} %constant_dynamic-update-slice_fusion.tok_ref, bf16[80,128,128]{2,1,0:T(8,128)(2,1)} %collective-permute-done.9.rest_0_, ...), custom_call_target="tpu_custom_call", output_to_operand_aliasing={{}: (5, {})} | custom-call | flops 262144 | bytes 262144 | tf_op jit(solution)/shard_map/block/pallas_call | solution.py:158
  349.9 20.0 %block.14.rest_4_ = f32[2,512,4096]{2,1,0:T(8,128)} custom-call(s32[1024]{0:T(1024)} %bitcast_select_fusion.codes_ref, s32[2]{0:T(128)} %pad_add_fusion.5.info_ref, bf16[512,4096]{1,0:T(8,128)(2,1)} %constant_dynamic-update-slice_fusion.tok_ref, bf16[80,128,128]{2,1,0:T(8,128)(2,1)} %copy-done.1, ...), custom_call_target="tpu_custom_call", output_to_operand_aliasing={{}: (5, {})} | custom-call | flops 262144 | bytes 262144 | tf_op jit(solution)/shard_map/block/pallas_call | solution.py:158
  369.9 0.9 collective-permute-start.20
  370.8 0.1 collective-permute-start.21
  370.9 0.7 pad_add_fusion.info_ref
  371.5 2.1 collective-permute-done.20.rest_2_
  373.7 1.9 collective-permute-done.21.rest_3_
  375.6 1.1 copy-done.5
  376.7 17.4 %block.15 = bf16[512,4096]{1,0:T(8,128)(2,1)} custom-call(s32[1024]{0:T(1024)} %bitcast_select_fusion.codes_ref, s32[2]{0:T(128)} %pad_add_fusion.info_ref, bf16[512,4096]{1,0:T(8,128)(2,1)} %constant_dynamic-update-slice_fusion.tok_ref, bf16[40,128,128]{2,1,0:T(8,128)(2,1)} %collective-permute-done.15.rest_0_, ...), custom_call_target="tpu_custom_call" | custom-call | flops 262144 | bytes 262144 | tf_op jit(solution)/shard_map/block/pallas_call | solution.py:158
  394.1 3.6 collective-permute-start.22
  397.7 46.4 %collective-permute-done.22 = bf16[512,4096]{1,0:T(8,128)(2,1)S(1)} collective-permute-done((bf16[512,4096]{1,0:T(8,128)(2,1)}, bf16[512,4096]{1,0:T(8,128)(2,1)S(1)}, u32[]{:S(2)}, u32[]{:S(2)}) %collective-permute-start.22) | collective-permute-done | bytes 4194336 | tf_op jit(solution)/shard_map/ppermute | solution.py:98
  444.1 2.0 copy.20
  (31 shorter events, 0.1 us)
Async XLA Ops:
  11.0 5.1 %collective-permute-start.2 = (bf16[80,128,128]{2,1,0:T(8,128)(2,1)}, bf16[80,128,128]{2,1,0:T(8,128)(2,1)S(1)}, u32[]{:S(2)}, u32[]{:S(2)}) collective-permute-start(bf16[80,128,128]{2,1,0:T(8,128)(2,1)} %get-tuple-element.21), channel_id=1, source_target_pairs={{0,1},{1,0},{2,3},{3,2},{4,5},{5,4},{6,7},{7,6},{8,9},{9,8},{10,11... | collective-permute-start | bytes 7864328 | tf_op jit(solution)/shard_map/ppermute | solution.py:98
  16.1 1.5 copy-start.3
  17.6 8.8 %copy-start.6 = (bf16[512,1024]{1,0:T(8,128)(2,1)S(1)}, bf16[512,1024]{1,0:T(8,128)(2,1)}, u32[]{:S(2)}) copy-start(bf16[512,1024]{1,0:T(8,128)(2,1)} %param.4) | copy-start | bytes 3145732
  20.6 148.1 %copy-start = (bf16[80,128,128]{2,1,0:T(8,128)(2,1)}, bf16[80,128,128]{2,1,0:T(8,128)(2,1)S(1)}, u32[]{:S(2)}) copy-start(bf16[80,128,128]{2,1,0:T(8,128)(2,1)S(1)} %get-tuple-element.40.rest_0_) | copy-start | bytes 7864324
  20.6 116.6 %collective-permute-start.3 = (bf16[80,128,128]{2,1,0:T(8,128)(2,1)S(1)}, bf16[80,128,128]{2,1,0:T(8,128)(2,1)}, u32[]{:S(2)}, u32[]{:S(2)}) collective-permute-start(bf16[80,128,128]{2,1,0:T(8,128)(2,1)S(1)} %get-tuple-element.40.rest_0_), channel_id=1, source_target_pairs={{0,16},{1,17},{2,18},{3,19},{4,20},{5,21},{6,22},{7,23},{8,24},{9,... | collective-permute-start | bytes 7864328 | tf_op jit(solution)/shard_map/ppermute | solution.py:98
  23.9 113.3 %collective-permute-start.4 = (bf16[80,128,128]{2,1,0:T(8,128)(2,1)S(1)}, bf16[80,128,128]{2,1,0:T(8,128)(2,1)}, u32[]{:S(2)}, u32[]{:S(2)}) collective-permute-start(bf16[80,128,128]{2,1,0:T(8,128)(2,1)S(1)} %get-tuple-element.39), channel_id=1, source_target_pairs={{0,8},{1,9},{2,10},{3,11},{4,12},{5,13},{6,14},{7,15},{8,0},{9,1},... | collective-permute-start | bytes 7864328 | tf_op jit(solution)/shard_map/ppermute | solution.py:98
  25.2 133.8 %collective-permute-start.5 = (bf16[80,128,128]{2,1,0:T(8,128)(2,1)S(1)}, bf16[80,128,128]{2,1,0:T(8,128)(2,1)}, u32[]{:S(2)}, u32[]{:S(2)}) collective-permute-start(bf16[80,128,128]{2,1,0:T(8,128)(2,1)S(1)} %get-tuple-element.40.rest_0_), channel_id=1, source_target_pairs={{0,4},{1,5},{2,6},{3,7},{4,0},{5,1},{6,2},{7,3},{8,12},{9,13},{10,... | collective-permute-start | bytes 7864328 | tf_op jit(solution)/shard_map/ppermute | solution.py:98
  26.4 132.7 %collective-permute-start.1 = (bf16[512,1024]{1,0:T(8,128)(2,1)S(1)}, bf16[512,1024]{1,0:T(8,128)(2,1)S(1)}, u32[]{:S(2)}, u32[]{:S(2)}) collective-permute-start(bf16[512,1024]{1,0:T(8,128)(2,1)S(1)} %copy-done.6), channel_id=1, source_target_pairs={{0,8},{1,9},{2,10},{3,11},{4,12},{5,13},{6,14},{7,15},{8,0},{9,1},... | collective-permute-start | bytes 3145736 | tf_op jit(solution)/shard_map/ppermute | solution.py:98
  160.6 5.6 %collective-permute-start.6 = (bf16[512,1024]{1,0:T(8,128)(2,1)}, bf16[512,1024]{1,0:T(8,128)(2,1)}, u32[]{:S(2)}, u32[]{:S(2)}) collective-permute-start(bf16[512,1024]{1,0:T(8,128)(2,1)} %get-tuple-element.41), channel_id=1, source_target_pairs={{0,1},{1,0},{2,3},{3,2},{4,5},{5,4},{6,7},{7,6},{8,9},{9,8},{10,11... | collective-permute-start | bytes 3145736 | tf_op jit(solution)/shard_map/ppermute | solution.py:98
  162.1 13.2 %collective-permute-start.14 = (bf16[80,128,128]{2,1,0:T(8,128)(2,1)S(1)}, bf16[80,128,128]{2,1,0:T(8,128)(2,1)}, u32[]{:S(2)}, u32[]{:S(2)}) collective-permute-start(bf16[80,128,128]{2,1,0:T(8,128)(2,1)S(1)} %get-tuple-element.40.rest_0_), channel_id=1, source_target_pairs={{0,1},{1,0},{2,3},{3,2},{4,5},{5,4},{6,7},{7,6},{8,9},{9,8},{10,11... | collective-permute-start | bytes 7864328 | tf_op jit(solution)/shard_map/ppermute | solution.py:98
  162.1 14.2 %collective-permute-start.13 = (bf16[80,128,128]{2,1,0:T(8,128)(2,1)}, bf16[80,128,128]{2,1,0:T(8,128)(2,1)}, u32[]{:S(2)}, u32[]{:S(2)}) collective-permute-start(bf16[80,128,128]{2,1,0:T(8,128)(2,1)} %collective-permute-done.5.rest_0_), channel_id=1, source_target_pairs={{0,1},{1,0},{2,3},{3,2},{4,5},{5,4},{6,7},{7,6},{8,9},{9,8},{10,11... | collective-permute-start | bytes 7864328 | tf_op jit(solution)/shard_map/ppermute | solution.py:98
  162.6 6.1 %copy-start.2 = (bf16[512,1024]{1,0:T(8,128)(2,1)S(1)}, bf16[512,1024]{1,0:T(8,128)(2,1)}, u32[]{:S(2)}) copy-start(bf16[512,1024]{1,0:T(8,128)(2,1)} %get-tuple-element.42) | copy-start | bytes 3145732
  168.7 4.7 %copy-start.7 = (s32[32,32]{1,0:T(8,128)S(1)}, s32[32,32]{1,0:T(8,128)}, u32[]{:S(2)}) copy-start(s32[32,32]{1,0:T(8,128)} %param.7) | copy-start | bytes 12292
  172.0 46.9 %collective-permute-start.7 = (bf16[512,2048]{1,0:T(8,128)(2,1)S(1)}, bf16[512,2048]{1,0:T(8,128)(2,1)}, u32[]{:S(2)}, u32[]{:S(2)}) collective-permute-start(bf16[512,2048]{1,0:T(8,128)(2,1)S(1)} %get-tuple-element.36), channel_id=1, source_target_pairs={{0,2},{1,3},{2,0},{3,1},{4,6},{5,7},{6,4},{7,5},{8,10},{9,11},{10,... | collective-permute-start | bytes 6291464 | tf_op jit(solution)/shard_map/ppermute | solution.py:98
  173.4 1.5 collective-permute-start
  174.0 86.9 %collective-permute-start.12 = (bf16[80,128,128]{2,1,0:T(8,128)(2,1)}, bf16[80,128,128]{2,1,0:T(8,128)(2,1)}, u32[]{:S(2)}, u32[]{:S(2)}) collective-permute-start(bf16[80,128,128]{2,1,0:T(8,128)(2,1)} %collective-permute-done.4.rest_0_), channel_id=1, source_target_pairs={{0,1},{1,0},{2,3},{3,2},{4,5},{5,4},{6,7},{7,6},{8,9},{9,8},{10,11... | collective-permute-start | bytes 7864328 | tf_op jit(solution)/shard_map/ppermute | solution.py:98
  174.9 106.1 %collective-permute-start.11 = (bf16[80,128,128]{2,1,0:T(8,128)(2,1)}, bf16[80,128,128]{2,1,0:T(8,128)(2,1)}, u32[]{:S(2)}, u32[]{:S(2)}) collective-permute-start(bf16[80,128,128]{2,1,0:T(8,128)(2,1)} %collective-permute-done.3.rest_0_), channel_id=1, source_target_pairs={{0,1},{1,0},{2,3},{3,2},{4,5},{5,4},{6,7},{7,6},{8,9},{9,8},{10,11... | collective-permute-start | bytes 7864328 | tf_op jit(solution)/shard_map/ppermute | solution.py:98
  175.2 125.8 %collective-permute-start.10 = (bf16[80,128,128]{2,1,0:T(8,128)(2,1)}, bf16[80,128,128]{2,1,0:T(8,128)(2,1)S(1)}, u32[]{:S(2)}, u32[]{:S(2)}) collective-permute-start(bf16[80,128,128]{2,1,0:T(8,128)(2,1)} %collective-permute-done.4.rest_0_), channel_id=1, source_target_pairs={{0,16},{1,17},{2,18},{3,19},{4,20},{5,21},{6,22},{7,23},{8,24},{9,... | collective-permute-start | bytes 7864328 | tf_op jit(solution)/shard_map/ppermute | solution.py:98
  176.2 124.8 %collective-permute-start.8 = (bf16[80,128,128]{2,1,0:T(8,128)(2,1)}, bf16[80,128,128]{2,1,0:T(8,128)(2,1)}, u32[]{:S(2)}, u32[]{:S(2)}) collective-permute-start(bf16[80,128,128]{2,1,0:T(8,128)(2,1)} %collective-permute-done.3.rest_0_), channel_id=1, source_target_pairs={{0,4},{1,5},{2,6},{3,7},{4,0},{5,1},{6,2},{7,3},{8,12},{9,13},{10,... | collective-permute-start | bytes 7864328 | tf_op jit(solution)/shard_map/ppermute | solution.py:98
  218.9 82.2 %collective-permute-start.9 = (bf16[80,128,128]{2,1,0:T(8,128)(2,1)}, bf16[80,128,128]{2,1,0:T(8,128)(2,1)}, u32[]{:S(2)}, u32[]{:S(2)}) collective-permute-start(bf16[80,128,128]{2,1,0:T(8,128)(2,1)} %collective-permute-done.4.rest_0_), channel_id=1, source_target_pairs={{0,4},{1,5},{2,6},{3,7},{4,0},{5,1},{6,2},{7,3},{8,12},{9,13},{10,... | collective-permute-start | bytes 7864328 | tf_op jit(solution)/shard_map/ppermute | solution.py:98
  301.1 5.7 %copy-start.1 = (bf16[80,128,128]{2,1,0:T(8,128)(2,1)}, bf16[80,128,128]{2,1,0:T(8,128)(2,1)S(1)}, u32[]{:S(2)}) copy-start(bf16[80,128,128]{2,1,0:T(8,128)(2,1)S(1)} %collective-permute-done.10.rest_0_) | copy-start | bytes 7864324
  301.1 8.7 %collective-permute-start.19 = (bf16[80,128,128]{2,1,0:T(8,128)(2,1)}, bf16[80,128,128]{2,1,0:T(8,128)(2,1)}, u32[]{:S(2)}, u32[]{:S(2)}) collective-permute-start(bf16[80,128,128]{2,1,0:T(8,128)(2,1)} %collective-permute-done.8.rest_0_), channel_id=1, source_target_pairs={{0,1},{1,0},{2,3},{3,2},{4,5},{5,4},{6,7},{7,6},{8,9},{9,8},{10,11... | collective-permute-start | bytes 7864328 | tf_op jit(solution)/shard_map/ppermute | solution.py:98
  302.5 27.3 %collective-permute-start.18 = (bf16[80,128,128]{2,1,0:T(8,128)(2,1)}, bf16[80,128,128]{2,1,0:T(8,128)(2,1)}, u32[]{:S(2)}, u32[]{:S(2)}) collective-permute-start(bf16[80,128,128]{2,1,0:T(8,128)(2,1)} %collective-permute-done.9.rest_0_), channel_id=1, source_target_pairs={{0,1},{1,0},{2,3},{3,2},{4,5},{5,4},{6,7},{7,6},{8,9},{9,8},{10,11... | collective-permute-start | bytes 7864328 | tf_op jit(solution)/shard_map/ppermute | solution.py:98
  302.6 47.3 %collective-permute-start.17 = (bf16[80,128,128]{2,1,0:T(8,128)(2,1)S(1)}, bf16[80,128,128]{2,1,0:T(8,128)(2,1)}, u32[]{:S(2)}, u32[]{:S(2)}) collective-permute-start(bf16[80,128,128]{2,1,0:T(8,128)(2,1)S(1)} %collective-permute-done.10.rest_0_), channel_id=1, source_target_pairs={{0,1},{1,0},{2,3},{3,2},{4,5},{5,4},{6,7},{7,6},{8,9},{9,8},{10,11... | collective-permute-start | bytes 7864328 | tf_op jit(solution)/shard_map/ppermute | solution.py:98
  306.7 63.2 %collective-permute-start.15 = (bf16[40,128,128]{2,1,0:T(8,128)(2,1)}, bf16[40,128,128]{2,1,0:T(8,128)(2,1)}, u32[]{:S(2)}, u32[]{:S(2)}) collective-permute-start(bf16[40,128,128]{2,1,0:T(8,128)(2,1)} %slice.6), channel_id=1, source_target_pairs={{0,4},{1,5},{2,6},{3,7},{4,0},{5,1},{6,2},{7,3},{8,12},{9,13},{10,... | collective-permute-start | bytes 3932168 | tf_op jit(solution)/shard_map/ppermute | solution.py:98
  306.7 63.2 %collective-permute-start.16 = (bf16[40,128,128]{2,1,0:T(8,128)(2,1)}, bf16[40,128,128]{2,1,0:T(8,128)(2,1)}, u32[]{:S(2)}, u32[]{:S(2)}) collective-permute-start(bf16[40,128,128]{2,1,0:T(8,128)(2,1)} %slice.7), channel_id=1, source_target_pairs={{0,16},{1,17},{2,18},{3,19},{4,20},{5,21},{6,22},{7,23},{8,24},{9,... | collective-permute-start | bytes 3932168 | tf_op jit(solution)/shard_map/ppermute | solution.py:98
  369.9 3.7 collective-permute-start.20
  370.8 4.7 %collective-permute-start.21 = (bf16[40,128,128]{2,1,0:T(8,128)(2,1)}, bf16[40,128,128]{2,1,0:T(8,128)(2,1)S(1)}, u32[]{:S(2)}, u32[]{:S(2)}) collective-permute-start(bf16[40,128,128]{2,1,0:T(8,128)(2,1)} %collective-permute-done.16.rest_1_), channel_id=1, source_target_pairs={{0,1},{1,0},{2,3},{3,2},{4,5},{5,4},{6,7},{7,6},{8,9},{9,8},{10,11... | collective-permute-start | bytes 3932168 | tf_op jit(solution)/shard_map/ppermute | solution.py:98
  373.7 1.9 copy-start.4
  375.6 1.1 copy-start.5
  394.1 50.0 %collective-permute-start.22 = (bf16[512,4096]{1,0:T(8,128)(2,1)}, bf16[512,4096]{1,0:T(8,128)(2,1)S(1)}, u32[]{:S(2)}, u32[]{:S(2)}) collective-permute-start(bf16[512,4096]{1,0:T(8,128)(2,1)} %block.15), channel_id=1, source_target_pairs={{0,0},{1,8},{2,2},{3,10},{4,4},{5,12},{6,6},{7,14},{8,1},{9,9},{10... | collective-permute-start | bytes 12582920 | tf_op jit(solution)/shard_map/ppermute | solution.py:98

commit v3 on v2

v3 whole, which is shorter than its diff:
```python
import functools

import jax
import jax.numpy as jnp
from jax import lax
from jax.experimental import pallas as pl
from jax.experimental.pallas import tpu as pltpu
from jax.sharding import PartitionSpec as P

TILE = 128
VMEM_LIMIT = 56 * 1024 * 1024


def pack_kernel(row_tiles, col_tiles, core_ref, mask_ref, gate_ref, up_ref, mine_ref, other_ref):
    core = core_ref[0]

    def tile_step(i, j, slot):
        kept = mask_ref[i * col_tiles + j]
        rows = pl.ds(i * TILE, TILE)
        cols = pl.ds(pl.multiple_of(j * TILE, TILE), TILE)

        @pl.when((kept == 1) & (core == 0))
        def _():
            mine_ref[slot] = gate_ref[rows, cols]
            other_ref[slot] = up_ref[rows, cols]

        @pl.when((kept == 1) & (core == 1))
        def _():
            mine_ref[slot] = up_ref[rows, cols]
            other_ref[slot] = gate_ref[rows, cols]

        return slot + kept

    slot = jnp.int32(0)
    for i in range(row_tiles):
        slot = lax.fori_loop(0, col_tiles, functools.partial(tile_step, i), slot)


def block_kernel(row_tiles, col_tiles, chunk_tiles, counts, first, last, codes_ref, info_ref, *rest):
    blocks = len(counts)
    tok_refs, rest = rest[:blocks], rest[blocks:]
    pieces, rest = rest[:2 * sum(counts)], rest[2 * sum(counts):]
    if first:
        acc_ref = None
    else:
        acc_ref, rest = rest[0], rest[1:]
    out_ref, packed, dense, sems = rest
    core = info_ref[blocks]
    chunk = pl.program_id(0)

    @pl.when(chunk == 0)
    def _():
        copies = []
        for b in range(blocks):
            for kind in range(2):
                start = 0
                for _ in range(counts[b]):
                    ref = pieces[len(copies)]
                    copies.append(pltpu.make_async_copy(
                        ref, packed.at[b, kind, pl.ds(start, ref.shape[0])], sems.at[len(copies)]))
                    start += ref.shape[0]
        for copy in copies:
            copy.start()
        for copy in copies:
            copy.wait()

    sums = []
    for kind in range(2):
        total = None if first else acc_ref[kind]
        for b in range(blocks):
            for i in range(row_tiles):
                for j in range(chunk_tiles):
                    code = codes_ref[(info_ref[b] * row_tiles + i) * col_tiles + chunk * chunk_tiles + j]
                    tile = packed[b, kind, jnp.maximum(code, 0)]
                    dense[b, kind, pl.ds(i * TILE, TILE), pl.ds(j * TILE, TILE)] = jnp.where(
                        code >= 0, tile, jnp.zeros_like(tile))
            product = jnp.dot(tok_refs[b][...], dense[b, kind], preferred_element_type=jnp.float32)
            total = product if total is None else total + product
        if last:
            sums.append(total)
        else:
            out_ref[kind] = total
    if last:
        gate = jnp.where(core == 0, sums[0], sums[1])
        up = jnp.where(core == 0, sums[1], sums[0])
        out_ref[...] = (gate / (1.0 + jnp.exp(-gate)) * up).astype(out_ref.dtype)


def solution(mesh):
    R, C = mesh.shape["row"], mesh.shape["col"]
    NZ = R // 2
    axes = ("row", "col")

    def send(value, move):
        pairs = []
        for r in range(R):
            for c in range(C):
                tr, tc = move(r, c)
                pairs.append((r * C + c, tr * C + tc))
        return lax.ppermute(value, axes, pairs)

    sibling = lambda r, c: (r, c ^ 1)
    z_pair = lambda r, c: (r ^ 2, c)
    x_pair = lambda r, c: (r ^ 1, c)

    def swap_out(r, c):
        return (r, c) if ((r // 2) % 2) == (c % 2) else (r ^ 2, c ^ 1)

    def on_device(tokens, gate_weight, up_weight, tile_mask):
        depth, cols = gate_weight.shape
        row_tiles, col_tiles = depth // TILE, cols // TILE
        slots = 5 * row_tiles * col_tiles // 8
        rows = tokens.shape[0]
        r = lax.axis_index("row")
        core = lax.axis_index("col") % 2
        home = ((r // 2) % 2) == core

        def after(value, acc):
            return lax.optimization_barrier((value, acc))

        tok_other = send(tokens, z_pair)
        smem = pl.BlockSpec(memory_space=pltpu.SMEM)
        vmem = pl.BlockSpec(memory_space=pltpu.VMEM)
        own_mask = lax.dynamic_slice_in_dim(tile_mask, r * row_tiles, row_tiles, 0).reshape(-1)
        piece = jax.ShapeDtypeStruct((slots, TILE, TILE), gate_weight.dtype)
        mine, other = pl.pallas_call(
            functools.partial(pack_kernel, row_tiles, col_tiles),
            out_shape=(piece, piece),
            in_specs=[smem, smem, vmem, vmem],
            out_specs=(vmem, vmem),
            compiler_params=pltpu.CompilerParams(vmem_limit_bytes=VMEM_LIMIT),
            name="pack",
        )(core.reshape(1).astype(jnp.int32), own_mask, gate_weight, up_weight)

        mask_sib = send(tile_mask, sibling)
        job_mask = jnp.where(home, tile_mask, mask_sib).reshape(R, row_tiles * col_tiles)
        place = jnp.arange(row_tiles * col_tiles)
        upto = (place[None, :] <= place[:, None]).astype(jnp.int32)
        slot = jnp.sum(job_mask[:, None, :] * upto[None], axis=2) - 1
        codes = jnp.where(job_mask == 1, slot, -1).reshape(-1)

        crossed, tok_other = after(send(other, sibling), tok_other)
        keep = jnp.where(home, mine, crossed)
        give = jnp.where(home, crossed, mine)
        chunk_tiles = min(4, col_tiles)
        width = chunk_tiles * TILE

        def add_blocks(acc, todo, last=False):
            first = acc is None
            counts = tuple(len(values) for values, _ in todo)
            info = jnp.stack([block for _, block in todo] + [core]).astype(jnp.int32)
            acc_spec = pl.BlockSpec((2, rows, width), lambda g, *_: (0, 0, g))
            in_specs = [pl.BlockSpec((rows, depth), lambda g, codes, info, b=b: (0, info[b]))
                        for b in range(len(todo))]
            operands = [codes, info] + [tok] * len(todo)
            for values, _ in todo:
                operands += [v for v, _ in values] + [w for _, w in values]
            in_specs += [pl.BlockSpec(memory_space=pl.ANY)] * (2 * sum(counts))
            if not first:
                in_specs.append(acc_spec)
                operands.append(acc)
            if last:
                out_shape = jax.ShapeDtypeStruct((rows, cols), jnp.bfloat16)
                out_spec = pl.BlockSpec((rows, width), lambda g, *_: (0, g))
            else:
                out_shape = jax.ShapeDtypeStruct((2, rows, cols), jnp.float32)
                out_spec = acc_spec
            return pl.pallas_call(
                functools.partial(block_kernel, row_tiles, col_tiles, chunk_tiles, counts, first, last),
                out_shape=out_shape,
                grid_spec=pltpu.PrefetchScalarGridSpec(
                    num_scalar_prefetch=2,
                    grid=(cols // width,),
                    in_specs=in_specs,
                    out_specs=out_spec,
                    scratch_shapes=[pltpu.VMEM((len(todo), 2, slots, TILE, TILE), jnp.bfloat16),
                                    pltpu.VMEM((len(todo), 2, depth, width), jnp.bfloat16),
                                    pltpu.SemaphoreType.DMA((2 * sum(counts),))],
                ),
                input_output_aliases={} if first or last else {len(operands) - 1: 0},
                compiler_params=pltpu.CompilerParams(vmem_limit_bytes=VMEM_LIMIT),
                cost_estimate=pl.CostEstimate(
                    flops=rows * depth, bytes_accessed=rows * depth, transcendentals=0),
                name="block",
            )(*operands)

        def along(value, s):
            return send(value, lambda rr, cc: ((rr + 4 * s) % R, cc))

        def with_sibling(value):
            return (value, send(value, sibling))

        paired = send(give, z_pair)
        far = [along(keep, s) for s in range(1, NZ // 2)]
        tok_mine = jnp.where(home, tokens, tok_other)
        tok_sib = send(jnp.where(home, tok_other, tokens), sibling)
        wide = tokens.shape[1]
        both = jnp.where(core == 0, jnp.concatenate([tok_mine, tok_sib], 1),
                         jnp.concatenate([tok_sib, tok_mine], 1))
        y = lax.axis_index("col") // 2
        tok_parts = [send(both, lambda rr, cc, s=s: (rr, (cc + 2 * s) % C)) for s in range(1, C // 2)]
        keep_x = send(keep, x_pair)
        (tok_parts, keep_x), (far, paired) = after((tok_parts, keep_x), (far, paired))
        tok = jnp.zeros((rows, wide * C), tokens.dtype)
        tok = lax.dynamic_update_slice_in_dim(tok, both, y * 2 * wide, 1)
        for s, part in enumerate(tok_parts, 1):
            source = (y - s) % (C // 2)
            tok = lax.dynamic_update_slice_in_dim(tok, part, source * 2 * wide, 1)
        half = slots // 2
        acc = add_blocks(None, [([with_sibling(keep)], r), ([with_sibling(keep_x)], r ^ 1)])
        far_paired = [along(paired, s) for s in range(1, NZ // 2)]
        far_x = [send(value, x_pair) for value in far]
        paired_x = send(paired, x_pair)
        todo = [([with_sibling(paired)], r ^ 2)]
        for s, value in enumerate(far, 1):
            todo.append(([with_sibling(value)], (r - 4 * s) % R))
        for n in range(0, len(todo), 2):
            acc = add_blocks(acc, todo[n:n + 2])
        far_paired, acc = after(far_paired, acc)
        (far_x, paired_x), far_paired = after((far_x, paired_x), far_paired)
        last_a = [send(value[:half], x_pair) for value in far_paired]
        last_b = [along(paired_x[half:], s) for s in range(1, NZ // 2)]
        todo = [([with_sibling(paired_x)], r ^ 3)]
        for s, value in enumerate(far_x, 1):
            todo.append(([with_sibling(value)], ((r - 4 * s) % R) ^ 1))
        for s, value in enumerate(far_paired, 1):
            todo.append(([with_sibling(value)], ((r ^ 2) - 4 * s) % R))
        for n in range(0, len(todo), 2):
            acc = add_blocks(acc, todo[n:n + 2])
        (last_a, last_b), acc = after((last_a, last_b), acc)
        for s in range(1, NZ // 2):
            acc = add_blocks(acc, [([with_sibling(last_a[s - 1]), with_sibling(last_b[s - 1])],
                                    (((r ^ 2) - 4 * s) % R) ^ 1)], last=s == NZ // 2 - 1)
        return send(acc, swap_out)

    placed = (P("row", "col"), P("row", "col"), P("row", "col"), P(None, "col"))
    return jax.shard_map(
        on_device, mesh=mesh, in_specs=placed, out_specs=P("row", "col"), check_vma=False
    )
```

time: 447 us -> 427 us (0.955)
  Pallas kernels: 161 us -> 112 us
  waiting for transfers between devices: 234 us -> 262 us
    pallas_call x8 -> x5, Pallas kernels: 151 us -> 103 us  [add_blocks(): pl.pallas_call(functools.partial(block_kernel, row_tiles, col_tiles, chun...]
    ppermute x23, waiting for transfers between devices: 234 us -> 262 us  [send(): return lax.ppermute(value, axes, pairs)]
  transfers between devices with their start and end apart: 23 -> 23, of which waited for: 9 -> 12; matrix products, arithmetic and copies ran while one was open for 4% -> 5% of each run, Pallas kernels for 30% -> 20%
where the time goes in v3:
time: 427 us; the launch traced here: 425 us
  waiting for transfers between devices  262 us (61%)
  Pallas kernels  112 us (26%)
  starting transfers between devices  20.1 us (5%)
  local copies, waits for them, and re-layouts  16.6 us (4%)
  other arithmetic  14.9 us (3%)
    ppermute x23, waiting for transfers between devices, send(): return lax.ppermute(value, axes, pairs)  262 us
    pallas_call x5, Pallas kernels, add_blocks(): pl.pallas_call(functools.partial(block_kernel, row_tiles, col_tiles, chun...  103 us
    ppermute x23, starting transfers between devices, send(): return lax.ppermute(value, axes, pairs)  20.1 us
    pallas_call x1, Pallas kernels, on_device(): pl.pallas_call(functools.partial(pack_kernel, row_tiles, col_tiles), out_...  9.23 us
  transfers between devices with their start and end apart: 23, of which 12 were waited for; matrix products, arithmetic and copies ran while one was open for 5% of the time, Pallas kernels for 20%

profile of v3, /device:TPU:1, one launch (start us, length us, event | category | flops | bytes accessed | tf_op | source)
XLA Modules:
  0.0 425.3 jit_solution(4712227409218317970)
XLA Ops:
  0.0 0.7 constant_dynamic-slice_fusion
  0.7 0.6 reshape.26.mask_ref
  1.3 9.2 %pack.1 = (bf16[80,128,128]{2,1,0:T(8,128)(2,1)}, bf16[80,128,128]{2,1,0:T(8,128)(2,1)}) custom-call(s32[1]{0:T(128)} %bitcast.2.core_ref, s32[128]{0:T(128)} %reshape.26.mask_ref, bf16[512,4096]{1,0:T(8,128)(2,1)} %gate_ref.1, bf16[512,4096]{1,0:T(8,128)(2,1)} %up_ref.1), custom_call_target="tpu_custom_call" | custom-call | tf_op jit(solution)/shard_map/pack/pallas_call | solution.py:126
  10.5 0.4 collective-permute-start.1
  10.9 2.4 collective-permute-start.2
  13.3 23.7 %collective-permute-done.2 = bf16[512,1024]{1,0:T(8,128)(2,1)} collective-permute-done((bf16[512,1024]{1,0:T(8,128)(2,1)}, bf16[512,1024]{1,0:T(8,128)(2,1)}, u32[]{:S(2)}, u32[]{:S(2)}) %collective-permute-start.2) | collective-permute-done | bytes 1048608 | tf_op jit(solution)/shard_map/ppermute | solution.py:100
  37.0 3.9 broadcast_select_fusion.2
  41.0 0.7 collective-permute-start.3
  41.7 3.9 broadcast_select_fusion
  45.6 1.5 collective-permute-start.5
  47.1 2.2 collective-permute-start.6
  49.3 1.3 collective-permute-start.7
  50.6 0.0 collective-permute-done.3
  50.6 2.5 broadcast_in_dim.3
  53.2 3.2 constant_dynamic-update-slice_fusion.1
  56.4 1.2 collective-permute-start.4
  57.6 1.1 collective-permute-start.13
  58.7 45.7 %collective-permute-done.5.rest_4_ = bf16[80,128,128]{2,1,0:T(8,128)(2,1)} collective-permute-done((bf16[80,128,128]{2,1,0:T(8,128)(2,1)S(1)}, bf16[80,128,128]{2,1,0:T(8,128)(2,1)}, u32[]{:S(2)}, u32[]{:S(2)}) %collective-permute-start.5) | collective-permute-done | bytes 2621472 | tf_op jit(solution)/shard_map/ppermute | solution.py:100
  104.3 58.2 %collective-permute-done.6.rest_4_ = bf16[80,128,128]{2,1,0:T(8,128)(2,1)} collective-permute-done((bf16[80,128,128]{2,1,0:T(8,128)(2,1)S(1)}, bf16[80,128,128]{2,1,0:T(8,128)(2,1)}, u32[]{:S(2)}, u32[]{:S(2)}) %collective-permute-start.6) | collective-permute-done | bytes 2621472 | tf_op jit(solution)/shard_map/ppermute | solution.py:100
  162.5 0.0 collective-permute-done.7.rest_2_
  162.5 0.0 collective-permute-done.4
  162.5 1.6 collective-permute-start.14
  164.1 0.1 collective-permute-start
  164.2 0.4 collective-permute-start.11
  164.6 0.1 collective-permute-start.12
  164.7 3.9 collective-permute-done
  168.6 0.7 collective-permute-start.10
  169.2 0.3 collective-permute-start.8
  169.5 1.2 copy-done.3
  170.7 1.2 collective-permute-done.14.rest_5_
  171.9 1.5 copy-done.4
  173.4 0.6 add_add_fusion.1.info_ref
  174.0 0.1 mul.26
  174.1 0.1 eq.23
  174.2 0.2 multiply_reduce_fusion
  174.4 0.6 bitcast_select_fusion.codes_ref
  175.0 3.2 constant_dynamic-update-slice_fusion.rest_0_.rest_1_
  178.1 0.6 add_add_fusion.info_ref
  178.7 19.3 %block.5.rest_6_ = f32[2,512,4096]{2,1,0:T(8,128)} custom-call(s32[1024]{0:T(1024)} %bitcast_select_fusion.codes_ref, s32[3]{0:T(128)} %add_add_fusion.1.info_ref, bf16[512,4096]{1,0:T(8,128)(2,1)} %constant_dynamic-update-slice_fusion.rest_0_.rest_1_, bf16[512,4096]{1,0:T(8,128)(2,1)} %constant_dynamic-update-slice_fusion.rest_0_.rest_1_, ...), custom_call_target="tpu_custom_call" | custom-call | flops 262144 | bytes 262144 | tf_op jit(solution)/shard_map/block/pallas_call | solution.py:168
  198.0 23.0 %block.6.rest_6_ = f32[2,512,4096]{2,1,0:T(8,128)} custom-call(s32[1024]{0:T(1024)} %bitcast_select_fusion.codes_ref, s32[3]{0:T(128)} %add_add_fusion.info_ref, bf16[512,4096]{1,0:T(8,128)(2,1)} %constant_dynamic-update-slice_fusion.rest_0_.rest_1_, ...), custom_call_target="tpu_custom_call", output_to_operand_aliasing={{}: (8, {})} | custom-call | flops 262144 | bytes 262144 | tf_op jit(solution)/shard_map/block/pallas_call | solution.py:168
  221.0 63.3 %collective-permute-done.10.rest_1_ = bf16[80,128,128]{2,1,0:T(8,128)(2,1)} collective-permute-done((bf16[80,128,128]{2,1,0:T(8,128)(2,1)}, bf16[80,128,128]{2,1,0:T(8,128)(2,1)}, u32[]{:S(2)}, u32[]{:S(2)}) %collective-permute-start.10) | collective-permute-done | bytes 2621472 | tf_op jit(solution)/shard_map/ppermute | solution.py:100
  284.3 1.0 collective-permute-start.18
  285.3 0.1 collective-permute-start.19
  285.4 0.4 collective-permute-start.17
  285.8 2.5 slice.6
  288.4 1.2 slice.7
  289.5 1.3 collective-permute-start.16
  290.8 0.6 pad_add_fusion.1.info_ref
  291.4 0.6 add_add_fusion.2.info_ref
  292.0 0.9 collective-permute-done.18.rest_3_
  292.9 1.0 collective-permute-done.19.rest_5_
  294.0 23.0 %block.7.rest_3_ = f32[2,512,4096]{2,1,0:T(8,128)} custom-call(s32[1024]{0:T(1024)} %bitcast_select_fusion.codes_ref, s32[3]{0:T(128)} %add_add_fusion.2.info_ref, bf16[512,4096]{1,0:T(8,128)(2,1)} %constant_dynamic-update-slice_fusion.rest_0_.rest_1_, ...), custom_call_target="tpu_custom_call", output_to_operand_aliasing={{}: (8, {})} | custom-call | flops 262144 | bytes 262144 | tf_op jit(solution)/shard_map/block/pallas_call | solution.py:168
  317.0 20.0 %block.8.rest_5_ = f32[2,512,4096]{2,1,0:T(8,128)} custom-call(s32[1024]{0:T(1024)} %bitcast_select_fusion.codes_ref, s32[2]{0:T(128)} %pad_add_fusion.1.info_ref, bf16[512,4096]{1,0:T(8,128)(2,1)} %constant_dynamic-update-slice_fusion.rest_0_.rest_1_, bf16[80,128,128]{2,1,0:T(8,128)(2,1)} %collective-permute-done.10.rest_1_, ...), custom_call_target="tpu_custom_call", output_to_operand_aliasing={{}: (5, {})} | custom-call | flops 262144 | bytes 262144 | tf_op jit(solution)/shard_map/block/pallas_call | solution.py:168
  336.9 11.7 %collective-permute-done.16.rest_2_ = bf16[40,128,128]{2,1,0:T(8,128)(2,1)} collective-permute-done((bf16[40,128,128]{2,1,0:T(8,128)(2,1)}, bf16[40,128,128]{2,1,0:T(8,128)(2,1)}, u32[]{:S(2)}, u32[]{:S(2)}) %collective-permute-start.16) | collective-permute-done | bytes 1310752 | tf_op jit(solution)/shard_map/ppermute | solution.py:100
  348.6 1.4 collective-permute-start.20
  350.0 0.0 collective-permute-start.21
  350.0 0.6 pad_add_fusion.info_ref
  350.7 2.2 collective-permute-done.20.rest_3_
  352.9 1.9 collective-permute-done.21.rest_4_
  354.8 1.1 copy-done.8
  355.9 17.4 %block.9 = bf16[512,4096]{1,0:T(8,128)(2,1)} custom-call(s32[1024]{0:T(1024)} %bitcast_select_fusion.codes_ref, s32[2]{0:T(128)} %pad_add_fusion.info_ref, bf16[512,4096]{1,0:T(8,128)(2,1)} %constant_dynamic-update-slice_fusion.rest_0_.rest_1_, bf16[40,128,128]{2,1,0:T(8,128)(2,1)} %collective-permute-done.15.rest_1_, ...), custom_call_target="tpu_custom_call" | custom-call | flops 262144 | bytes 262144 | tf_op jit(solution)/shard_map/block/pallas_call | solution.py:168
  373.2 1.9 collective-permute-start.22
  375.2 48.1 %collective-permute-done.22 = bf16[512,4096]{1,0:T(8,128)(2,1)S(1)} collective-permute-done((bf16[512,4096]{1,0:T(8,128)(2,1)}, bf16[512,4096]{1,0:T(8,128)(2,1)S(1)}, u32[]{:S(2)}, u32[]{:S(2)}) %collective-permute-start.22) | collective-permute-done | bytes 4194336 | tf_op jit(solution)/shard_map/ppermute | solution.py:100
  423.3 2.0 copy.14
  (29 shorter events, 0.1 us)
Async XLA Ops:
  10.5 26.5 %collective-permute-start.1 = (bf16[80,128,128]{2,1,0:T(8,128)(2,1)}, bf16[80,128,128]{2,1,0:T(8,128)(2,1)S(1)}, u32[]{:S(2)}, u32[]{:S(2)}) collective-permute-start(bf16[80,128,128]{2,1,0:T(8,128)(2,1)} %get-tuple-element.21), channel_id=1, source_target_pairs={{0,1},{1,0},{2,3},{3,2},{4,5},{5,4},{6,7},{7,6},{8,9},{9,8},{10,11... | collective-permute-start | bytes 7864328 | tf_op jit(solution)/shard_map/ppermute | solution.py:100
  10.9 26.1 %collective-permute-start.2 = (bf16[512,1024]{1,0:T(8,128)(2,1)}, bf16[512,1024]{1,0:T(8,128)(2,1)}, u32[]{:S(2)}, u32[]{:S(2)}) collective-permute-start(bf16[512,1024]{1,0:T(8,128)(2,1)} %param.4), channel_id=1, source_target_pairs={{0,8},{1,9},{2,10},{3,11},{4,12},{5,13},{6,14},{7,15},{8,0},{9,1},... | collective-permute-start | bytes 3145736 | tf_op jit(solution)/shard_map/ppermute | solution.py:100
  13.3 28.4 %copy-start.5 = (bf16[80,128,128]{2,1,0:T(8,128)(2,1)S(1)}, bf16[80,128,128]{2,1,0:T(8,128)(2,1)}, u32[]{:S(2)}) copy-start(bf16[80,128,128]{2,1,0:T(8,128)(2,1)} %get-tuple-element.23) | copy-start | bytes 7864324
  37.0 4.6 %copy-start.6 = (bf16[80,128,128]{2,1,0:T(8,128)(2,1)}, bf16[80,128,128]{2,1,0:T(8,128)(2,1)S(1)}, u32[]{:S(2)}) copy-start(bf16[80,128,128]{2,1,0:T(8,128)(2,1)S(1)} %collective-permute-done.1) | copy-start | bytes 7864324
  41.0 9.7 %collective-permute-start.3 = (bf16[512,1024]{1,0:T(8,128)(2,1)}, bf16[512,1024]{1,0:T(8,128)(2,1)}, u32[]{:S(2)}, u32[]{:S(2)}) collective-permute-start(bf16[512,1024]{1,0:T(8,128)(2,1)} %get-tuple-element.43), channel_id=1, source_target_pairs={{0,1},{1,0},{2,3},{3,2},{4,5},{5,4},{6,7},{7,6},{8,9},{9,8},{10,11... | collective-permute-start | bytes 3145736 | tf_op jit(solution)/shard_map/ppermute | solution.py:100
  45.6 12.0 %copy-start = (bf16[80,128,128]{2,1,0:T(8,128)(2,1)}, bf16[80,128,128]{2,1,0:T(8,128)(2,1)S(1)}, u32[]{:S(2)}) copy-start(bf16[80,128,128]{2,1,0:T(8,128)(2,1)S(1)} %get-tuple-element.42.rest_2_) | copy-start | bytes 7864324
  45.6 58.8 %collective-permute-start.5 = (bf16[80,128,128]{2,1,0:T(8,128)(2,1)S(1)}, bf16[80,128,128]{2,1,0:T(8,128)(2,1)}, u32[]{:S(2)}, u32[]{:S(2)}) collective-permute-start(bf16[80,128,128]{2,1,0:T(8,128)(2,1)S(1)} %get-tuple-element.42.rest_2_), channel_id=1, source_target_pairs={{0,4},{1,5},{2,6},{3,7},{4,0},{5,1},{6,2},{7,3},{8,12},{9,13},{10,... | collective-permute-start | bytes 7864328 | tf_op jit(solution)/shard_map/ppermute | solution.py:100
  47.1 115.4 %collective-permute-start.6 = (bf16[80,128,128]{2,1,0:T(8,128)(2,1)S(1)}, bf16[80,128,128]{2,1,0:T(8,128)(2,1)}, u32[]{:S(2)}, u32[]{:S(2)}) collective-permute-start(bf16[80,128,128]{2,1,0:T(8,128)(2,1)S(1)} %get-tuple-element.42.rest_2_), channel_id=1, source_target_pairs={{0,16},{1,17},{2,18},{3,19},{4,20},{5,21},{6,22},{7,23},{8,24},{9,... | collective-permute-start | bytes 7864328 | tf_op jit(solution)/shard_map/ppermute | solution.py:100
  49.3 113.2 %collective-permute-start.7 = (bf16[80,128,128]{2,1,0:T(8,128)(2,1)}, bf16[80,128,128]{2,1,0:T(8,128)(2,1)}, u32[]{:S(2)}, u32[]{:S(2)}) collective-permute-start(bf16[80,128,128]{2,1,0:T(8,128)(2,1)} %get-tuple-element.41), channel_id=1, source_target_pairs={{0,8},{1,9},{2,10},{3,11},{4,12},{5,13},{6,14},{7,15},{8,0},{9,1},... | collective-permute-start | bytes 7864328 | tf_op jit(solution)/shard_map/ppermute | solution.py:100
  50.6 2.5 copy-start.2
  53.2 111.0 %copy-start.9 = (s32[32,32]{1,0:T(8,128)S(1)}, s32[32,32]{1,0:T(8,128)}, u32[]{:S(2)}) copy-start(s32[32,32]{1,0:T(8,128)} %param.7) | copy-start | bytes 12292
  56.4 106.1 %collective-permute-start.4 = (bf16[512,2048]{1,0:T(8,128)(2,1)S(1)}, bf16[512,2048]{1,0:T(8,128)(2,1)}, u32[]{:S(2)}, u32[]{:S(2)}) collective-permute-start(bf16[512,2048]{1,0:T(8,128)(2,1)S(1)} %get-tuple-element.38), channel_id=1, source_target_pairs={{0,2},{1,3},{2,0},{3,1},{4,6},{5,7},{6,4},{7,5},{8,10},{9,11},{10,... | collective-permute-start | bytes 6291464 | tf_op jit(solution)/shard_map/ppermute | solution.py:100
  57.6 111.7 %collective-permute-start.13 = (bf16[80,128,128]{2,1,0:T(8,128)(2,1)S(1)}, bf16[80,128,128]{2,1,0:T(8,128)(2,1)S(1)}, u32[]{:S(2)}, u32[]{:S(2)}) collective-permute-start(bf16[80,128,128]{2,1,0:T(8,128)(2,1)S(1)} %get-tuple-element.42.rest_2_), channel_id=1, source_target_pairs={{0,1},{1,0},{2,3},{3,2},{4,5},{5,4},{6,7},{7,6},{8,9},{9,8},{10,11... | collective-permute-start | bytes 7864328 | tf_op jit(solution)/shard_map/ppermute | solution.py:100
  162.5 9.4 %collective-permute-start.14 = (bf16[80,128,128]{2,1,0:T(8,128)(2,1)}, bf16[80,128,128]{2,1,0:T(8,128)(2,1)S(1)}, u32[]{:S(2)}, u32[]{:S(2)}) collective-permute-start(bf16[80,128,128]{2,1,0:T(8,128)(2,1)} %collective-permute-done.5.rest_4_), channel_id=1, source_target_pairs={{0,1},{1,0},{2,3},{3,2},{4,5},{5,4},{6,7},{7,6},{8,9},{9,8},{10,11... | collective-permute-start | bytes 7864328 | tf_op jit(solution)/shard_map/ppermute | solution.py:100
  164.1 4.4 %collective-permute-start = (s32[32,32]{1,0:T(8,128)S(1)}, s32[32,32]{1,0:T(8,128)S(1)}, u32[]{:S(2)}, u32[]{:S(2)}) collective-permute-start(s32[32,32]{1,0:T(8,128)S(1)} %copy-done.9), channel_id=1, source_target_pairs={{0,1},{1,0},{2,3},{3,2},{4,5},{5,4},{6,7},{7,6},{8,9},{9,8},{10,11... | collective-permute-start | bytes 12296 | tf_op jit(solution)/shard_map/ppermute | solution.py:100
  164.2 33.8 %collective-permute-start.11 = (bf16[80,128,128]{2,1,0:T(8,128)(2,1)}, bf16[80,128,128]{2,1,0:T(8,128)(2,1)}, u32[]{:S(2)}, u32[]{:S(2)}) collective-permute-start(bf16[80,128,128]{2,1,0:T(8,128)(2,1)} %collective-permute-done.7.rest_2_), channel_id=1, source_target_pairs={{0,1},{1,0},{2,3},{3,2},{4,5},{5,4},{6,7},{7,6},{8,9},{9,8},{10,11... | collective-permute-start | bytes 7864328 | tf_op jit(solution)/shard_map/ppermute | solution.py:100
  164.6 33.4 %collective-permute-start.12 = (bf16[80,128,128]{2,1,0:T(8,128)(2,1)}, bf16[80,128,128]{2,1,0:T(8,128)(2,1)}, u32[]{:S(2)}, u32[]{:S(2)}) collective-permute-start(bf16[80,128,128]{2,1,0:T(8,128)(2,1)} %collective-permute-done.6.rest_4_), channel_id=1, source_target_pairs={{0,1},{1,0},{2,3},{3,2},{4,5},{5,4},{6,7},{7,6},{8,9},{9,8},{10,11... | collective-permute-start | bytes 7864328 | tf_op jit(solution)/shard_map/ppermute | solution.py:100
  168.6 115.7 %collective-permute-start.10 = (bf16[80,128,128]{2,1,0:T(8,128)(2,1)}, bf16[80,128,128]{2,1,0:T(8,128)(2,1)}, u32[]{:S(2)}, u32[]{:S(2)}) collective-permute-start(bf16[80,128,128]{2,1,0:T(8,128)(2,1)} %collective-permute-done.7.rest_2_), channel_id=1, source_target_pairs={{0,16},{1,17},{2,18},{3,19},{4,20},{5,21},{6,22},{7,23},{8,24},{9,... | collective-permute-start | bytes 7864328 | tf_op jit(solution)/shard_map/ppermute | solution.py:100
  169.2 1.5 copy-start.3
  169.2 115.1 %collective-permute-start.8 = (bf16[80,128,128]{2,1,0:T(8,128)(2,1)}, bf16[80,128,128]{2,1,0:T(8,128)(2,1)}, u32[]{:S(2)}, u32[]{:S(2)}) collective-permute-start(bf16[80,128,128]{2,1,0:T(8,128)(2,1)} %collective-permute-done.6.rest_4_), channel_id=1, source_target_pairs={{0,4},{1,5},{2,6},{3,7},{4,0},{5,1},{6,2},{7,3},{8,12},{9,13},{10,... | collective-permute-start | bytes 7864328 | tf_op jit(solution)/shard_map/ppermute | solution.py:100
  171.9 1.5 copy-start.4
  173.4 110.9 %collective-permute-start.9 = (bf16[80,128,128]{2,1,0:T(8,128)(2,1)}, bf16[80,128,128]{2,1,0:T(8,128)(2,1)S(1)}, u32[]{:S(2)}, u32[]{:S(2)}) collective-permute-start(bf16[80,128,128]{2,1,0:T(8,128)(2,1)} %collective-permute-done.7.rest_2_), channel_id=1, source_target_pairs={{0,4},{1,5},{2,6},{3,7},{4,0},{5,1},{6,2},{7,3},{8,12},{9,13},{10,... | collective-permute-start | bytes 7864328 | tf_op jit(solution)/shard_map/ppermute | solution.py:100
  284.3 5.2 %copy-start.1 = (bf16[80,128,128]{2,1,0:T(8,128)(2,1)}, bf16[80,128,128]{2,1,0:T(8,128)(2,1)S(1)}, u32[]{:S(2)}) copy-start(bf16[80,128,128]{2,1,0:T(8,128)(2,1)S(1)} %collective-permute-done.9.rest_2_) | copy-start | bytes 7864324
  284.3 8.6 %collective-permute-start.18 = (bf16[80,128,128]{2,1,0:T(8,128)(2,1)S(1)}, bf16[80,128,128]{2,1,0:T(8,128)(2,1)}, u32[]{:S(2)}, u32[]{:S(2)}) collective-permute-start(bf16[80,128,128]{2,1,0:T(8,128)(2,1)S(1)} %collective-permute-done.9.rest_2_), channel_id=1, source_target_pairs={{0,1},{1,0},{2,3},{3,2},{4,5},{5,4},{6,7},{7,6},{8,9},{9,8},{10,11... | collective-permute-start | bytes 7864328 | tf_op jit(solution)/shard_map/ppermute | solution.py:100
  285.3 8.6 %collective-permute-start.19 = (bf16[80,128,128]{2,1,0:T(8,128)(2,1)}, bf16[80,128,128]{2,1,0:T(8,128)(2,1)}, u32[]{:S(2)}, u32[]{:S(2)}) collective-permute-start(bf16[80,128,128]{2,1,0:T(8,128)(2,1)} %collective-permute-done.8.rest_4_), channel_id=1, source_target_pairs={{0,1},{1,0},{2,3},{3,2},{4,5},{5,4},{6,7},{7,6},{8,9},{9,8},{10,11... | collective-permute-start | bytes 7864328 | tf_op jit(solution)/shard_map/ppermute | solution.py:100
  285.4 31.5 %collective-permute-start.17 = (bf16[80,128,128]{2,1,0:T(8,128)(2,1)}, bf16[80,128,128]{2,1,0:T(8,128)(2,1)}, u32[]{:S(2)}, u32[]{:S(2)}) collective-permute-start(bf16[80,128,128]{2,1,0:T(8,128)(2,1)} %collective-permute-done.10.rest_1_), channel_id=1, source_target_pairs={{0,1},{1,0},{2,3},{3,2},{4,5},{5,4},{6,7},{7,6},{8,9},{9,8},{10,11... | collective-permute-start | bytes 7864328 | tf_op jit(solution)/shard_map/ppermute | solution.py:100
  289.5 47.4 %collective-permute-start.15 = (bf16[40,128,128]{2,1,0:T(8,128)(2,1)}, bf16[40,128,128]{2,1,0:T(8,128)(2,1)}, u32[]{:S(2)}, u32[]{:S(2)}) collective-permute-start(bf16[40,128,128]{2,1,0:T(8,128)(2,1)} %slice.6), channel_id=1, source_target_pairs={{0,4},{1,5},{2,6},{3,7},{4,0},{5,1},{6,2},{7,3},{8,12},{9,13},{10,... | collective-permute-start | bytes 3932168 | tf_op jit(solution)/shard_map/ppermute | solution.py:100
  289.5 59.1 %collective-permute-start.16 = (bf16[40,128,128]{2,1,0:T(8,128)(2,1)}, bf16[40,128,128]{2,1,0:T(8,128)(2,1)}, u32[]{:S(2)}, u32[]{:S(2)}) collective-permute-start(bf16[40,128,128]{2,1,0:T(8,128)(2,1)} %slice.7), channel_id=1, source_target_pairs={{0,16},{1,17},{2,18},{3,19},{4,20},{5,21},{6,22},{7,23},{8,24},{9,... | collective-permute-start | bytes 3932168 | tf_op jit(solution)/shard_map/ppermute | solution.py:100
  348.6 4.3 %collective-permute-start.20 = (bf16[40,128,128]{2,1,0:T(8,128)(2,1)}, bf16[40,128,128]{2,1,0:T(8,128)(2,1)S(1)}, u32[]{:S(2)}, u32[]{:S(2)}) collective-permute-start(bf16[40,128,128]{2,1,0:T(8,128)(2,1)} %collective-permute-done.15.rest_1_), channel_id=1, source_target_pairs={{0,1},{1,0},{2,3},{3,2},{4,5},{5,4},{6,7},{7,6},{8,9},{9,8},{10,11... | collective-permute-start | bytes 3932168 | tf_op jit(solution)/shard_map/ppermute | solution.py:100
  350.0 4.7 %collective-permute-start.21 = (bf16[40,128,128]{2,1,0:T(8,128)(2,1)}, bf16[40,128,128]{2,1,0:T(8,128)(2,1)S(1)}, u32[]{:S(2)}, u32[]{:S(2)}) collective-permute-start(bf16[40,128,128]{2,1,0:T(8,128)(2,1)} %collective-permute-done.16.rest_2_), channel_id=1, source_target_pairs={{0,1},{1,0},{2,3},{3,2},{4,5},{5,4},{6,7},{7,6},{8,9},{9,8},{10,11... | collective-permute-start | bytes 3932168 | tf_op jit(solution)/shard_map/ppermute | solution.py:100
  352.9 1.9 copy-start.7
  354.8 1.1 copy-start.8
  373.2 50.0 %collective-permute-start.22 = (bf16[512,4096]{1,0:T(8,128)(2,1)}, bf16[512,4096]{1,0:T(8,128)(2,1)S(1)}, u32[]{:S(2)}, u32[]{:S(2)}) collective-permute-start(bf16[512,4096]{1,0:T(8,128)(2,1)} %block.9), channel_id=1, source_target_pairs={{0,0},{1,8},{2,2},{3,10},{4,4},{5,12},{6,6},{7,14},{8,1},{9,9},{10... | collective-permute-start | bytes 12582920 | tf_op jit(solution)/shard_map/ppermute | solution.py:100

commit v4 on v3

--- a/solution.py
+++ b/solution.py
@@ -206,7 +206,7 @@
         for s, part in enumerate(tok_parts, 1):
             source = (y - s) % (C // 2)
             tok = lax.dynamic_update_slice_in_dim(tok, part, source * 2 * wide, 1)
-        half = slots // 2
+        half = 2 * slots // 3
         acc = add_blocks(None, [([with_sibling(keep)], r), ([with_sibling(keep_x)], r ^ 1)])
         far_paired = [along(paired, s) for s in range(1, NZ // 2)]
         far_x = [send(value, x_pair) for value in far]

time: 427 us -> 415 us (0.972)
  waiting for transfers between devices: 262 us -> 247 us
    ppermute x23, waiting for transfers between devices: 262 us -> 247 us  [send(): return lax.ppermute(value, axes, pairs)]
  transfers between devices with their start and end apart: 23 -> 23, of which waited for: 12 -> 11; matrix products, arithmetic and copies ran while one was open for 5% -> 5% of each run, Pallas kernels for 20% -> 21%
where the time goes in v4:
time: 415 us; the launch traced here: 414 us
  waiting for transfers between devices  247 us (60%)
  Pallas kernels  112 us (27%)
  starting transfers between devices  22.9 us (6%)
  local copies, waits for them, and re-layouts  17 us (4%)
  other arithmetic  15 us (4%)
    ppermute x23, waiting for transfers between devices, send(): return lax.ppermute(value, axes, pairs)  247 us
    pallas_call x5, Pallas kernels, add_blocks(): pl.pallas_call(functools.partial(block_kernel, row_tiles, col_tiles, chun...  103 us
    ppermute x23, starting transfers between devices, send(): return lax.ppermute(value, axes, pairs)  22.9 us
    pallas_call x1, Pallas kernels, on_device(): pl.pallas_call(functools.partial(pack_kernel, row_tiles, col_tiles), out_...  9.23 us
  transfers between devices with their start and end apart: 23, of which 11 were waited for; matrix products, arithmetic and copies ran while one was open for 5% of the time, Pallas kernels for 21%

profile of v4, /device:TPU:1, one launch (start us, length us, event | category | flops | bytes accessed | tf_op | source)
XLA Modules:
  0.0 414.0 jit_solution(4173825817639964889)
XLA Ops:
  0.0 0.7 constant_dynamic-slice_fusion
  0.7 0.6 reshape.26.mask_ref
  1.3 9.2 %pack.1 = (bf16[80,128,128]{2,1,0:T(8,128)(2,1)}, bf16[80,128,128]{2,1,0:T(8,128)(2,1)}) custom-call(s32[1]{0:T(128)} %bitcast.2.core_ref, s32[128]{0:T(128)} %reshape.26.mask_ref, bf16[512,4096]{1,0:T(8,128)(2,1)} %gate_ref.1, bf16[512,4096]{1,0:T(8,128)(2,1)} %up_ref.1), custom_call_target="tpu_custom_call" | custom-call | tf_op jit(solution)/shard_map/pack/pallas_call | solution.py:126
  10.5 0.4 collective-permute-start.1
  10.9 2.6 collective-permute-start.2
  13.4 23.8 %collective-permute-done.2 = bf16[512,1024]{1,0:T(8,128)(2,1)} collective-permute-done((bf16[512,1024]{1,0:T(8,128)(2,1)}, bf16[512,1024]{1,0:T(8,128)(2,1)}, u32[]{:S(2)}, u32[]{:S(2)}) %collective-permute-start.2) | collective-permute-done | bytes 1048608 | tf_op jit(solution)/shard_map/ppermute | solution.py:100
  37.3 3.9 broadcast_select_fusion.2
  41.2 0.6 collective-permute-start.3
  41.8 3.9 broadcast_select_fusion
  45.7 1.4 collective-permute-start.5
  47.1 2.2 collective-permute-start.6
  49.3 1.5 collective-permute-start.7
  50.8 0.0 collective-permute-done.3
  50.8 2.5 broadcast_in_dim.3
  53.3 3.2 constant_dynamic-update-slice_fusion.1
  56.5 1.0 collective-permute-start.4
  57.5 1.1 collective-permute-start.13
  58.7 45.7 %collective-permute-done.5.rest_4_ = bf16[80,128,128]{2,1,0:T(8,128)(2,1)} collective-permute-done((bf16[80,128,128]{2,1,0:T(8,128)(2,1)S(1)}, bf16[80,128,128]{2,1,0:T(8,128)(2,1)}, u32[]{:S(2)}, u32[]{:S(2)}) %collective-permute-start.5) | collective-permute-done | bytes 2621472 | tf_op jit(solution)/shard_map/ppermute | solution.py:100
  104.3 58.2 %collective-permute-done.6.rest_4_ = bf16[80,128,128]{2,1,0:T(8,128)(2,1)} collective-permute-done((bf16[80,128,128]{2,1,0:T(8,128)(2,1)S(1)}, bf16[80,128,128]{2,1,0:T(8,128)(2,1)}, u32[]{:S(2)}, u32[]{:S(2)}) %collective-permute-start.6) | collective-permute-done | bytes 2621472 | tf_op jit(solution)/shard_map/ppermute | solution.py:100
  162.5 1.3 collective-permute-start.14
  163.8 0.1 collective-permute-start
  163.9 0.4 collective-permute-start.11
  164.3 0.1 collective-permute-start.12
  164.4 3.9 collective-permute-done
  168.3 1.3 collective-permute-start.10
  169.5 0.2 collective-permute-start.8
  169.8 1.3 copy-done.3
  171.0 0.6 collective-permute-done.14.rest_5_
  171.6 1.5 copy-done.4
  173.1 0.7 collective-permute-start.9
  173.8 0.6 add_add_fusion.1.info_ref
  174.4 0.1 mul.26
  174.5 0.1 eq.23
  174.6 0.2 multiply_reduce_fusion
  174.8 0.6 bitcast_select_fusion.codes_ref
  175.4 3.2 constant_dynamic-update-slice_fusion.rest_0_.rest_1_
  178.5 0.6 add_add_fusion.info_ref
  179.1 19.3 %block.5.rest_6_ = f32[2,512,4096]{2,1,0:T(8,128)} custom-call(s32[1024]{0:T(1024)} %bitcast_select_fusion.codes_ref, s32[3]{0:T(128)} %add_add_fusion.1.info_ref, bf16[512,4096]{1,0:T(8,128)(2,1)} %constant_dynamic-update-slice_fusion.rest_0_.rest_1_, bf16[512,4096]{1,0:T(8,128)(2,1)} %constant_dynamic-update-slice_fusion.rest_0_.rest_1_, ...), custom_call_target="tpu_custom_call" | custom-call | flops 262144 | bytes 262144 | tf_op jit(solution)/shard_map/block/pallas_call | solution.py:168
  198.4 23.0 %block.6.rest_6_ = f32[2,512,4096]{2,1,0:T(8,128)} custom-call(s32[1024]{0:T(1024)} %bitcast_select_fusion.codes_ref, s32[3]{0:T(128)} %add_add_fusion.info_ref, bf16[512,4096]{1,0:T(8,128)(2,1)} %constant_dynamic-update-slice_fusion.rest_0_.rest_1_, ...), custom_call_target="tpu_custom_call", output_to_operand_aliasing={{}: (8, {})} | custom-call | flops 262144 | bytes 262144 | tf_op jit(solution)/shard_map/block/pallas_call | solution.py:168
  221.4 62.6 %collective-permute-done.10.rest_1_ = bf16[80,128,128]{2,1,0:T(8,128)(2,1)} collective-permute-done((bf16[80,128,128]{2,1,0:T(8,128)(2,1)}, bf16[80,128,128]{2,1,0:T(8,128)(2,1)}, u32[]{:S(2)}, u32[]{:S(2)}) %collective-permute-start.10) | collective-permute-done | bytes 2621472 | tf_op jit(solution)/shard_map/ppermute | solution.py:100
  284.0 0.1 collective-permute-done.9.rest_2_
  284.1 1.2 collective-permute-start.18
  285.2 0.0 collective-permute-start.19
  285.2 0.5 collective-permute-start.17
  285.7 2.9 slice.6
  288.6 0.5 collective-permute-start.15
  289.1 0.1 slice.7
  289.2 1.4 collective-permute-start.16
  290.6 0.7 pad_add_fusion.1.info_ref
  291.2 0.6 add_add_fusion.2.info_ref
  291.8 1.8 collective-permute-done.18.rest_3_
  293.6 0.3 collective-permute-done.19.rest_5_
  293.8 23.0 %block.7.rest_3_ = f32[2,512,4096]{2,1,0:T(8,128)} custom-call(s32[1024]{0:T(1024)} %bitcast_select_fusion.codes_ref, s32[3]{0:T(128)} %add_add_fusion.2.info_ref, bf16[512,4096]{1,0:T(8,128)(2,1)} %constant_dynamic-update-slice_fusion.rest_0_.rest_1_, ...), custom_call_target="tpu_custom_call", output_to_operand_aliasing={{}: (8, {})} | custom-call | flops 262144 | bytes 262144 | tf_op jit(solution)/shard_map/block/pallas_call | solution.py:168
  316.8 20.0 %block.8.rest_5_ = f32[2,512,4096]{2,1,0:T(8,128)} custom-call(s32[1024]{0:T(1024)} %bitcast_select_fusion.codes_ref, s32[2]{0:T(128)} %pad_add_fusion.1.info_ref, bf16[512,4096]{1,0:T(8,128)(2,1)} %constant_dynamic-update-slice_fusion.rest_0_.rest_1_, bf16[80,128,128]{2,1,0:T(8,128)(2,1)} %collective-permute-done.10.rest_1_, ...), custom_call_target="tpu_custom_call", output_to_operand_aliasing={{}: (5, {})} | custom-call | flops 262144 | bytes 262144 | tf_op jit(solution)/shard_map/block/pallas_call | solution.py:168
  336.8 0.4 collective-permute-start.20
  337.3 0.1 collective-permute-start.21
  337.4 0.6 pad_add_fusion.info_ref
  338.0 4.0 collective-permute-done.21.rest_4_
  342.0 0.9 copy-done.8
  343.0 1.2 copy-done.7
  344.2 17.3 %block.9 = bf16[512,4096]{1,0:T(8,128)(2,1)} custom-call(s32[1024]{0:T(1024)} %bitcast_select_fusion.codes_ref, s32[2]{0:T(128)} %pad_add_fusion.info_ref, bf16[512,4096]{1,0:T(8,128)(2,1)} %constant_dynamic-update-slice_fusion.rest_0_.rest_1_, bf16[53,128,128]{2,1,0:T(8,128)(2,1)} %collective-permute-done.15.rest_1_, ...), custom_call_target="tpu_custom_call" | custom-call | flops 262144 | bytes 262144 | tf_op jit(solution)/shard_map/block/pallas_call | solution.py:168
  361.5 4.1 collective-permute-start.22
  365.6 46.4 %collective-permute-done.22 = bf16[512,4096]{1,0:T(8,128)(2,1)S(1)} collective-permute-done((bf16[512,4096]{1,0:T(8,128)(2,1)}, bf16[512,4096]{1,0:T(8,128)(2,1)S(1)}, u32[]{:S(2)}, u32[]{:S(2)}) %collective-permute-start.22) | collective-permute-done | bytes 4194336 | tf_op jit(solution)/shard_map/ppermute | solution.py:100
  412.0 2.0 copy.14
  (29 shorter events, 0.1 us)
Async XLA Ops:
  10.5 26.8 %collective-permute-start.1 = (bf16[80,128,128]{2,1,0:T(8,128)(2,1)}, bf16[80,128,128]{2,1,0:T(8,128)(2,1)S(1)}, u32[]{:S(2)}, u32[]{:S(2)}) collective-permute-start(bf16[80,128,128]{2,1,0:T(8,128)(2,1)} %get-tuple-element.21), channel_id=1, source_target_pairs={{0,1},{1,0},{2,3},{3,2},{4,5},{5,4},{6,7},{7,6},{8,9},{9,8},{10,11... | collective-permute-start | bytes 7864328 | tf_op jit(solution)/shard_map/ppermute | solution.py:100
  10.9 26.4 %collective-permute-start.2 = (bf16[512,1024]{1,0:T(8,128)(2,1)}, bf16[512,1024]{1,0:T(8,128)(2,1)}, u32[]{:S(2)}, u32[]{:S(2)}) collective-permute-start(bf16[512,1024]{1,0:T(8,128)(2,1)} %param.4), channel_id=1, source_target_pairs={{0,8},{1,9},{2,10},{3,11},{4,12},{5,13},{6,14},{7,15},{8,0},{9,1},... | collective-permute-start | bytes 3145736 | tf_op jit(solution)/shard_map/ppermute | solution.py:100
  13.4 28.4 %copy-start.5 = (bf16[80,128,128]{2,1,0:T(8,128)(2,1)S(1)}, bf16[80,128,128]{2,1,0:T(8,128)(2,1)}, u32[]{:S(2)}) copy-start(bf16[80,128,128]{2,1,0:T(8,128)(2,1)} %get-tuple-element.23) | copy-start | bytes 7864324
  37.3 4.5 %copy-start.6 = (bf16[80,128,128]{2,1,0:T(8,128)(2,1)}, bf16[80,128,128]{2,1,0:T(8,128)(2,1)S(1)}, u32[]{:S(2)}) copy-start(bf16[80,128,128]{2,1,0:T(8,128)(2,1)S(1)} %collective-permute-done.1) | copy-start | bytes 7864324
  41.2 9.5 %collective-permute-start.3 = (bf16[512,1024]{1,0:T(8,128)(2,1)}, bf16[512,1024]{1,0:T(8,128)(2,1)}, u32[]{:S(2)}, u32[]{:S(2)}) collective-permute-start(bf16[512,1024]{1,0:T(8,128)(2,1)} %get-tuple-element.43), channel_id=1, source_target_pairs={{0,1},{1,0},{2,3},{3,2},{4,5},{5,4},{6,7},{7,6},{8,9},{9,8},{10,11... | collective-permute-start | bytes 3145736 | tf_op jit(solution)/shard_map/ppermute | solution.py:100
  45.7 11.8 %copy-start = (bf16[80,128,128]{2,1,0:T(8,128)(2,1)}, bf16[80,128,128]{2,1,0:T(8,128)(2,1)S(1)}, u32[]{:S(2)}) copy-start(bf16[80,128,128]{2,1,0:T(8,128)(2,1)S(1)} %get-tuple-element.42.rest_2_) | copy-start | bytes 7864324
  45.7 58.6 %collective-permute-start.5 = (bf16[80,128,128]{2,1,0:T(8,128)(2,1)S(1)}, bf16[80,128,128]{2,1,0:T(8,128)(2,1)}, u32[]{:S(2)}, u32[]{:S(2)}) collective-permute-start(bf16[80,128,128]{2,1,0:T(8,128)(2,1)S(1)} %get-tuple-element.42.rest_2_), channel_id=1, source_target_pairs={{0,4},{1,5},{2,6},{3,7},{4,0},{5,1},{6,2},{7,3},{8,12},{9,13},{10,... | collective-permute-start | bytes 7864328 | tf_op jit(solution)/shard_map/ppermute | solution.py:100
  47.1 115.4 %collective-permute-start.6 = (bf16[80,128,128]{2,1,0:T(8,128)(2,1)S(1)}, bf16[80,128,128]{2,1,0:T(8,128)(2,1)}, u32[]{:S(2)}, u32[]{:S(2)}) collective-permute-start(bf16[80,128,128]{2,1,0:T(8,128)(2,1)S(1)} %get-tuple-element.42.rest_2_), channel_id=1, source_target_pairs={{0,16},{1,17},{2,18},{3,19},{4,20},{5,21},{6,22},{7,23},{8,24},{9,... | collective-permute-start | bytes 7864328 | tf_op jit(solution)/shard_map/ppermute | solution.py:100
  49.3 113.2 %collective-permute-start.7 = (bf16[80,128,128]{2,1,0:T(8,128)(2,1)}, bf16[80,128,128]{2,1,0:T(8,128)(2,1)}, u32[]{:S(2)}, u32[]{:S(2)}) collective-permute-start(bf16[80,128,128]{2,1,0:T(8,128)(2,1)} %get-tuple-element.41), channel_id=1, source_target_pairs={{0,8},{1,9},{2,10},{3,11},{4,12},{5,13},{6,14},{7,15},{8,0},{9,1},... | collective-permute-start | bytes 7864328 | tf_op jit(solution)/shard_map/ppermute | solution.py:100
  50.8 2.5 copy-start.2
  53.3 110.5 %copy-start.9 = (s32[32,32]{1,0:T(8,128)S(1)}, s32[32,32]{1,0:T(8,128)}, u32[]{:S(2)}) copy-start(s32[32,32]{1,0:T(8,128)} %param.7) | copy-start | bytes 12292
  56.5 106.0 %collective-permute-start.4 = (bf16[512,2048]{1,0:T(8,128)(2,1)S(1)}, bf16[512,2048]{1,0:T(8,128)(2,1)}, u32[]{:S(2)}, u32[]{:S(2)}) collective-permute-start(bf16[512,2048]{1,0:T(8,128)(2,1)S(1)} %get-tuple-element.38), channel_id=1, source_target_pairs={{0,2},{1,3},{2,0},{3,1},{4,6},{5,7},{6,4},{7,5},{8,10},{9,11},{10,... | collective-permute-start | bytes 6291464 | tf_op jit(solution)/shard_map/ppermute | solution.py:100
  57.5 112.0 %collective-permute-start.13 = (bf16[80,128,128]{2,1,0:T(8,128)(2,1)S(1)}, bf16[80,128,128]{2,1,0:T(8,128)(2,1)S(1)}, u32[]{:S(2)}, u32[]{:S(2)}) collective-permute-start(bf16[80,128,128]{2,1,0:T(8,128)(2,1)S(1)} %get-tuple-element.42.rest_2_), channel_id=1, source_target_pairs={{0,1},{1,0},{2,3},{3,2},{4,5},{5,4},{6,7},{7,6},{8,9},{9,8},{10,11... | collective-permute-start | bytes 7864328 | tf_op jit(solution)/shard_map/ppermute | solution.py:100
  162.5 9.0 %collective-permute-start.14 = (bf16[80,128,128]{2,1,0:T(8,128)(2,1)}, bf16[80,128,128]{2,1,0:T(8,128)(2,1)S(1)}, u32[]{:S(2)}, u32[]{:S(2)}) collective-permute-start(bf16[80,128,128]{2,1,0:T(8,128)(2,1)} %collective-permute-done.5.rest_4_), channel_id=1, source_target_pairs={{0,1},{1,0},{2,3},{3,2},{4,5},{5,4},{6,7},{7,6},{8,9},{9,8},{10,11... | collective-permute-start | bytes 7864328 | tf_op jit(solution)/shard_map/ppermute | solution.py:100
  163.8 4.4 %collective-permute-start = (s32[32,32]{1,0:T(8,128)S(1)}, s32[32,32]{1,0:T(8,128)S(1)}, u32[]{:S(2)}, u32[]{:S(2)}) collective-permute-start(s32[32,32]{1,0:T(8,128)S(1)} %copy-done.9), channel_id=1, source_target_pairs={{0,1},{1,0},{2,3},{3,2},{4,5},{5,4},{6,7},{7,6},{8,9},{9,8},{10,11... | collective-permute-start | bytes 12296 | tf_op jit(solution)/shard_map/ppermute | solution.py:100
  163.9 34.5 %collective-permute-start.11 = (bf16[80,128,128]{2,1,0:T(8,128)(2,1)}, bf16[80,128,128]{2,1,0:T(8,128)(2,1)}, u32[]{:S(2)}, u32[]{:S(2)}) collective-permute-start(bf16[80,128,128]{2,1,0:T(8,128)(2,1)} %collective-permute-done.7.rest_2_), channel_id=1, source_target_pairs={{0,1},{1,0},{2,3},{3,2},{4,5},{5,4},{6,7},{7,6},{8,9},{9,8},{10,11... | collective-permute-start | bytes 7864328 | tf_op jit(solution)/shard_map/ppermute | solution.py:100
  164.3 34.1 %collective-permute-start.12 = (bf16[80,128,128]{2,1,0:T(8,128)(2,1)}, bf16[80,128,128]{2,1,0:T(8,128)(2,1)}, u32[]{:S(2)}, u32[]{:S(2)}) collective-permute-start(bf16[80,128,128]{2,1,0:T(8,128)(2,1)} %collective-permute-done.6.rest_4_), channel_id=1, source_target_pairs={{0,1},{1,0},{2,3},{3,2},{4,5},{5,4},{6,7},{7,6},{8,9},{9,8},{10,11... | collective-permute-start | bytes 7864328 | tf_op jit(solution)/shard_map/ppermute | solution.py:100
  168.3 115.7 %collective-permute-start.10 = (bf16[80,128,128]{2,1,0:T(8,128)(2,1)}, bf16[80,128,128]{2,1,0:T(8,128)(2,1)}, u32[]{:S(2)}, u32[]{:S(2)}) collective-permute-start(bf16[80,128,128]{2,1,0:T(8,128)(2,1)} %collective-permute-done.7.rest_2_), channel_id=1, source_target_pairs={{0,16},{1,17},{2,18},{3,19},{4,20},{5,21},{6,22},{7,23},{8,24},{9,... | collective-permute-start | bytes 7864328 | tf_op jit(solution)/shard_map/ppermute | solution.py:100
  169.5 1.5 copy-start.3
  169.5 114.4 %collective-permute-start.8 = (bf16[80,128,128]{2,1,0:T(8,128)(2,1)}, bf16[80,128,128]{2,1,0:T(8,128)(2,1)}, u32[]{:S(2)}, u32[]{:S(2)}) collective-permute-start(bf16[80,128,128]{2,1,0:T(8,128)(2,1)} %collective-permute-done.6.rest_4_), channel_id=1, source_target_pairs={{0,4},{1,5},{2,6},{3,7},{4,0},{5,1},{6,2},{7,3},{8,12},{9,13},{10,... | collective-permute-start | bytes 7864328 | tf_op jit(solution)/shard_map/ppermute | solution.py:100
  171.6 1.5 copy-start.4
  173.1 111.0 %collective-permute-start.9 = (bf16[80,128,128]{2,1,0:T(8,128)(2,1)}, bf16[80,128,128]{2,1,0:T(8,128)(2,1)S(1)}, u32[]{:S(2)}, u32[]{:S(2)}) collective-permute-start(bf16[80,128,128]{2,1,0:T(8,128)(2,1)} %collective-permute-done.7.rest_2_), channel_id=1, source_target_pairs={{0,4},{1,5},{2,6},{3,7},{4,0},{5,1},{6,2},{7,3},{8,12},{9,13},{10,... | collective-permute-start | bytes 7864328 | tf_op jit(solution)/shard_map/ppermute | solution.py:100
  284.0 5.2 %copy-start.1 = (bf16[80,128,128]{2,1,0:T(8,128)(2,1)}, bf16[80,128,128]{2,1,0:T(8,128)(2,1)S(1)}, u32[]{:S(2)}) copy-start(bf16[80,128,128]{2,1,0:T(8,128)(2,1)S(1)} %collective-permute-done.9.rest_2_) | copy-start | bytes 7864324
  284.1 9.5 %collective-permute-start.18 = (bf16[80,128,128]{2,1,0:T(8,128)(2,1)S(1)}, bf16[80,128,128]{2,1,0:T(8,128)(2,1)}, u32[]{:S(2)}, u32[]{:S(2)}) collective-permute-start(bf16[80,128,128]{2,1,0:T(8,128)(2,1)S(1)} %collective-permute-done.9.rest_2_), channel_id=1, source_target_pairs={{0,1},{1,0},{2,3},{3,2},{4,5},{5,4},{6,7},{7,6},{8,9},{9,8},{10,11... | collective-permute-start | bytes 7864328 | tf_op jit(solution)/shard_map/ppermute | solution.py:100
  285.2 8.6 %collective-permute-start.19 = (bf16[80,128,128]{2,1,0:T(8,128)(2,1)}, bf16[80,128,128]{2,1,0:T(8,128)(2,1)}, u32[]{:S(2)}, u32[]{:S(2)}) collective-permute-start(bf16[80,128,128]{2,1,0:T(8,128)(2,1)} %collective-permute-done.8.rest_4_), channel_id=1, source_target_pairs={{0,1},{1,0},{2,3},{3,2},{4,5},{5,4},{6,7},{7,6},{8,9},{9,8},{10,11... | collective-permute-start | bytes 7864328 | tf_op jit(solution)/shard_map/ppermute | solution.py:100
  285.2 31.6 %collective-permute-start.17 = (bf16[80,128,128]{2,1,0:T(8,128)(2,1)}, bf16[80,128,128]{2,1,0:T(8,128)(2,1)}, u32[]{:S(2)}, u32[]{:S(2)}) collective-permute-start(bf16[80,128,128]{2,1,0:T(8,128)(2,1)} %collective-permute-done.10.rest_1_), channel_id=1, source_target_pairs={{0,1},{1,0},{2,3},{3,2},{4,5},{5,4},{6,7},{7,6},{8,9},{9,8},{10,11... | collective-permute-start | bytes 7864328 | tf_op jit(solution)/shard_map/ppermute | solution.py:100
  288.6 48.2 %collective-permute-start.15 = (bf16[53,128,128]{2,1,0:T(8,128)(2,1)}, bf16[53,128,128]{2,1,0:T(8,128)(2,1)}, u32[]{:S(2)}, u32[]{:S(2)}) collective-permute-start(bf16[53,128,128]{2,1,0:T(8,128)(2,1)} %slice.6), channel_id=1, source_target_pairs={{0,4},{1,5},{2,6},{3,7},{4,0},{5,1},{6,2},{7,3},{8,12},{9,13},{10,... | collective-permute-start | bytes 5210120 | tf_op jit(solution)/shard_map/ppermute | solution.py:100
  289.2 47.6 %collective-permute-start.16 = (bf16[27,128,128]{2,1,0:T(8,128)(2,1)S(1)}, bf16[27,128,128]{2,1,0:T(8,128)(2,1)}, u32[]{:S(2)}, u32[]{:S(2)}) collective-permute-start(bf16[27,128,128]{2,1,0:T(8,128)(2,1)S(1)} %slice.7), channel_id=1, source_target_pairs={{0,16},{1,17},{2,18},{3,19},{4,20},{5,21},{6,22},{7,23},{8,24},{9,... | collective-permute-start | bytes 2654216 | tf_op jit(solution)/shard_map/ppermute | solution.py:100
  336.8 5.2 %collective-permute-start.20 = (bf16[53,128,128]{2,1,0:T(8,128)(2,1)}, bf16[53,128,128]{2,1,0:T(8,128)(2,1)S(1)}, u32[]{:S(2)}, u32[]{:S(2)}) collective-permute-start(bf16[53,128,128]{2,1,0:T(8,128)(2,1)} %collective-permute-done.15.rest_1_), channel_id=1, source_target_pairs={{0,1},{1,0},{2,3},{3,2},{4,5},{5,4},{6,7},{7,6},{8,9},{9,8},{10,11... | collective-permute-start | bytes 5210120 | tf_op jit(solution)/shard_map/ppermute | solution.py:100
  337.3 4.7 %collective-permute-start.21 = (bf16[27,128,128]{2,1,0:T(8,128)(2,1)}, bf16[27,128,128]{2,1,0:T(8,128)(2,1)S(1)}, u32[]{:S(2)}, u32[]{:S(2)}) collective-permute-start(bf16[27,128,128]{2,1,0:T(8,128)(2,1)} %collective-permute-done.16.rest_2_), channel_id=1, source_target_pairs={{0,1},{1,0},{2,3},{3,2},{4,5},{5,4},{6,7},{7,6},{8,9},{9,8},{10,11... | collective-permute-start | bytes 2654216 | tf_op jit(solution)/shard_map/ppermute | solution.py:100
  342.0 1.0 copy-start.8
  343.0 1.2 copy-start.7
  361.5 50.5 %collective-permute-start.22 = (bf16[512,4096]{1,0:T(8,128)(2,1)}, bf16[512,4096]{1,0:T(8,128)(2,1)S(1)}, u32[]{:S(2)}, u32[]{:S(2)}) collective-permute-start(bf16[512,4096]{1,0:T(8,128)(2,1)} %block.9), channel_id=1, source_target_pairs={{0,0},{1,8},{2,2},{3,10},{4,4},{5,12},{6,6},{7,14},{8,1},{9,9},{10... | collective-permute-start | bytes 12582920 | tf_op jit(solution)/shard_map/ppermute | solution.py:100
